TPU v7x, 128 devices: a whole 4x4x4 slice. The times are simulated.
128 devices in a mesh: ctx: 16 (over y, x), head: 8 (over z, core).
Axes of the slice: x: 4, y: 4, z: 4, core: 2. Of those that a mesh axis runs over, the one named last changes fastest.
Arguments:
- routed_q: bfloat16 [8192, 1024], P('ctx', 'head'), may hold values from -16 to 16
- routed_k: bfloat16 [8192, 1024], P('ctx', 'head'), may hold values from -16 to 16
- routed_v: bfloat16 [8192, 1024], P('ctx', 'head'), may hold values from -6 to 6
- routed_grad: bfloat16 [8192, 1024], P('ctx', 'head'), may hold values from -6 to 6
- local_q: bfloat16 [8192, 1024], P('ctx', 'head'), may hold values from -16 to 16
- local_k: bfloat16 [8192, 1024], P('ctx', 'head'), may hold values from -16 to 16
- local_v: bfloat16 [8192, 1024], P('ctx', 'head'), may hold values from -6 to 6
- local_grad: bfloat16 [8192, 1024], P('ctx', 'head'), may hold values from -6 to 6
- clusters: int32 [8, 8192], P('head', 'ctx'), may hold values from 0 to 127, as said below
- cluster_slot: int32 [8, 128], P('head'), may hold values from 0 to 127, each once within a row
- rel_bias: float32 [128], replicated, may hold values from -4 to 4
Outputs:
- routed_out: bfloat16 [8192, 1024], P('ctx', 'head')
- routed_dq: bfloat16 [8192, 1024], P('ctx', 'head')
- routed_dk: bfloat16 [8192, 1024], P('ctx', 'head')
- routed_dv: bfloat16 [8192, 1024], P('ctx', 'head')
- centroids: float32 [8, 128, 128], P('head', 'ctx')
- local_out: bfloat16 [8192, 1024], P('ctx', 'head')
- local_dq: bfloat16 [8192, 1024], P('ctx', 'head')
- local_dk: bfloat16 [8192, 1024], P('ctx', 'head')
- local_dv: bfloat16 [8192, 1024], P('ctx', 'head')
- bias_grad: float32 [128], replicated
Inputs may be any that keep to these rules, and one draw needn't show every extreme that they name: `clusters`: among the 512 positions of one index of ctx, at most 8 name the same cluster for one routed head; for every routed head one cluster is named exactly 8 times on every index of ctx.
All inputs are finite; a program needn't handle non-finite values.
Results may differ from a plain program's by a relative error of at most 0.0077.
Values may be sent and summed in bfloat16 or wider, within the bound.
A program may use at most 64 MiB of HBM per device.

v0:
```python
import jax
import jax.numpy as jnp
from jax import lax
from jax.sharding import PartitionSpec as P

HEAD_DIM = 128
WINDOW = 128
CLUSTER_MEAN = 64


NEG = -1e30
EPSILON = 1e-06


def from_behind(block, axis, distance):
    devices = range(lax.axis_size(axis))
    route = [(i - distance, i) for i in devices if i - distance in devices]
    return lax.ppermute(block, axis, route)


def over_pieces(value, axis):
    blocks = lax.all_gather(value, axis)
    return blocks.sum(axis=0)


def sent_together(arrays, axis, split_dim, concat_dim, along):
    ends, at = ([], 0)
    for a in arrays[:-1]:
        at += a.shape[along]
        ends.append(at)
    both = jnp.concatenate(arrays, axis=along)
    return tuple(
        jnp.split(
            lax.all_to_all(both, axis, split_axis=split_dim, concat_axis=concat_dim, tiled=True),
            ends,
            axis=along,
        )
    )


def softmax_rows(query, keys, allowed, offset_bias):
    scaling = query.shape[-1] ** (-0.5)
    scores = (
        jnp.einsum("bmd,bnd->bmn", query, keys, preferred_element_type=jnp.float32) * scaling
        + offset_bias
    )
    scores = jnp.where(allowed, scores, NEG)
    row_max = jnp.max(scores, axis=-1, keepdims=True)
    exponent = jnp.exp(scores - row_max)
    return exponent / jnp.sum(exponent, axis=-1, keepdims=True)


def weighted_values(weights_low, values):
    return jnp.einsum(
        "bmn,bnd->bmd", weights_low, values, preferred_element_type=jnp.float32
    ).astype(jnp.bfloat16)


def attention_grads(attn_weights, weights_low, query, keys, values, cotangent):
    weight_grad = jnp.einsum("bmd,bnd->bmn", cotangent, values, preferred_element_type=jnp.float32)
    score_grad = attn_weights * (
        weight_grad - jnp.sum(attn_weights * weight_grad, axis=-1, keepdims=True)
    )
    score_grad_low = score_grad.astype(jnp.bfloat16)
    scaling = query.shape[-1] ** (-0.5)
    query_grad = (
        jnp.einsum("bmn,bnd->bmd", score_grad_low, keys, preferred_element_type=jnp.float32)
        * scaling
    )
    keys_grad = (
        jnp.einsum("bmn,bmd->bnd", score_grad_low, query, preferred_element_type=jnp.float32)
        * scaling
    )
    values_grad = jnp.einsum(
        "bmn,bmd->bnd", weights_low, cotangent, preferred_element_type=jnp.float32
    )
    return (query_grad, keys_grad, values_grad, score_grad)


def plan_routes(cluster_ids, slots, ctx_size, per_source, per_dev):
    total = cluster_ids.shape[0]
    cluster_count = slots.shape[0]
    counts = jnp.sum(
        (cluster_ids[:, None] == jnp.arange(cluster_count, dtype=jnp.int32)[None, :]).astype(
            jnp.int32
        ),
        axis=0,
    )
    sorted_pos = jnp.argsort(cluster_ids, stable=True)
    sorted_ids = cluster_ids[sorted_pos]
    starts = jnp.cumsum(counts) - counts
    rank_in = jnp.arange(total, dtype=jnp.int32) - starts[sorted_ids]
    targets = slots[sorted_ids]
    flat_slot = (targets % per_dev * ctx_size + targets // per_dev) * per_source + rank_in
    destination = jnp.zeros((total,), jnp.int32).at[sorted_pos].set(flat_slot)
    filled = jnp.zeros((cluster_count,), jnp.int32).at[slots].set(counts).reshape(ctx_size, per_dev)
    return (destination, filled)


def offset_table():
    row_index = jnp.arange(WINDOW, dtype=jnp.int32)[:, None]
    col_index = jnp.arange(2 * WINDOW, dtype=jnp.int32)[None, :]
    offset = WINDOW + row_index - col_index
    inside = (offset >= 0) & (offset < WINDOW)
    return (offset, inside)


def shards(
    routed_q,
    routed_k,
    routed_v,
    routed_grad,
    local_q,
    local_k,
    local_v,
    local_grad,
    clusters,
    cluster_slot,
    rel_bias,
):
    ctx_size = lax.axis_size("ctx")
    tokens = routed_q.shape[0]
    head_dim = HEAD_DIM
    heads_here = routed_q.shape[1] // head_dim
    per_dev = tokens // CLUSTER_MEAN
    per_source = 2 * CLUSTER_MEAN // ctx_size
    capacity = per_source * ctx_size
    destination, filled = jax.vmap(
        lambda ids_row, slot_row: plan_routes(ids_row, slot_row, ctx_size, per_source, per_dev)
    )(clusters, cluster_slot)

    def split_heads(array, count):
        return array.reshape(tokens, count, head_dim).transpose(1, 0, 2)

    def packed(array):

        def one_head(token_rows, where_to):
            holder = (
                jnp.zeros((per_dev * ctx_size * per_source, head_dim), token_rows.dtype)
                .at[where_to]
                .set(token_rows)
            )
            return holder.reshape(per_dev, ctx_size, per_source, head_dim)

        return jax.vmap(one_head)(split_heads(array, heads_here), destination)

    def blocks(array):
        return array.reshape(heads_here * per_dev, capacity, head_dim)

    def unblock(array):
        return array.reshape(heads_here, per_dev, ctx_size, per_source, head_dim)

    def unpack(array):
        flat_rows = array.reshape(heads_here, per_dev * ctx_size * per_source, head_dim)
        token_rows = jax.vmap(lambda rows_head, where_to: rows_head[where_to])(
            flat_rows, destination
        )
        return token_rows.transpose(1, 0, 2).reshape(tokens, heads_here * head_dim)

    send_query = packed(routed_q)
    send_keys = packed(routed_k)
    send_values = packed(routed_v)
    send_cot = packed(routed_grad)
    got_counts = lax.all_to_all(filled, "ctx", split_axis=1, concat_axis=1, tiled=True)
    live_slots = (
        jnp.arange(per_source, dtype=jnp.int32)[None, None, None, :]
        < jnp.transpose(got_counts, (0, 2, 1))[..., None]
    ).reshape(heads_here * per_dev, capacity)
    causal = jnp.arange(capacity)[:, None] >= jnp.arange(capacity)[None, :]
    allowed = live_slots[:, None, :] & causal[None] | jnp.eye(capacity, dtype=bool)[None]
    local_count = local_q.shape[1] // head_dim
    block_count = tokens // WINDOW
    tail_keys, tail_values = from_behind((local_k[-WINDOW:], local_v[-WINDOW:]), "ctx", 1)

    def key_frames(earlier, array):
        extended = (
            jnp.concatenate([earlier, array], 0)
            .reshape(tokens + WINDOW, local_count, head_dim)
            .transpose(1, 0, 2)
        )
        return jnp.concatenate(
            [
                extended[:, :-WINDOW].reshape(local_count, block_count, WINDOW, head_dim),
                extended[:, WINDOW:].reshape(local_count, block_count, WINDOW, head_dim),
            ],
            2,
        ).reshape(local_count * block_count, 2 * WINDOW, head_dim)

    def query_blocks(array):
        return split_heads(array, local_count).reshape(local_count * block_count, WINDOW, head_dim)

    offset, inside = offset_table()
    offset_bias = jnp.take(rel_bias, jnp.clip(offset, 0, WINDOW - 1))
    key_pos = (
        lax.axis_index("ctx") * tokens
        + jnp.arange(block_count, dtype=jnp.int32)[:, None, None] * WINDOW
        - WINDOW
        + jnp.arange(2 * WINDOW, dtype=jnp.int32)[None, None, :]
    )
    window_allowed = jnp.broadcast_to(
        inside[None] & (key_pos >= 0), (local_count, block_count, WINDOW, 2 * WINDOW)
    )
    window_allowed = window_allowed.reshape(local_count * block_count, WINDOW, 2 * WINDOW)
    local_query = query_blocks(local_q)
    local_cot = query_blocks(local_grad)
    frame_keys = key_frames(tail_keys, local_k)
    frame_values = key_frames(tail_values, local_v)
    window_weights = softmax_rows(local_query, frame_keys, window_allowed, offset_bias)
    window_low = window_weights.astype(jnp.bfloat16)
    local_output = weighted_values(window_low, frame_values)
    local_qgrad, local_kgrad, local_vgrad, window_sgrad = attention_grads(
        window_weights, window_low, local_query, frame_keys, frame_values, local_cot
    )

    def fold_frames(array):
        array = array.reshape(local_count, block_count, 2 * WINDOW, head_dim)
        earlier_half = array[:, :, :WINDOW].reshape(local_count, tokens, head_dim)
        later_half = array[:, :, WINDOW:].reshape(local_count, tokens, head_dim)
        return jnp.pad(earlier_half, ((0, 0), (0, WINDOW), (0, 0))) + jnp.pad(
            later_half, ((0, 0), (WINDOW, 0), (0, 0))
        )

    keys_folded = fold_frames(local_kgrad)
    values_folded = fold_frames(local_vgrad)
    next_keys, next_values = (
        from_behind(keys_folded[:, :WINDOW].astype(jnp.bfloat16), "ctx", -1).astype(jnp.float32),
        from_behind(values_folded[:, :WINDOW].astype(jnp.bfloat16), "ctx", -1).astype(jnp.float32),
    )
    own_keys = keys_folded[:, WINDOW:].at[:, -WINDOW:].add(next_keys)
    own_values = values_folded[:, WINDOW:].at[:, -WINDOW:].add(next_values)

    def merge_local(array):
        return (
            array.reshape(local_count, tokens, head_dim)
            .transpose(1, 0, 2)
            .reshape(tokens, local_count * head_dim)
            .astype(jnp.bfloat16)
        )

    segment_ids = jnp.where(inside, offset, WINDOW).reshape(-1)
    score_total = jnp.sum(window_sgrad, axis=0)
    bias_part = jax.ops.segment_sum(score_total.reshape(-1), segment_ids, num_segments=WINDOW + 1)[
        :WINDOW
    ]
    bias_grad = over_pieces(bias_part, ("ctx", "head"))
    query_at, keys_at, values_at, cot_at = sent_together(
        (send_query, send_keys, send_values, send_cot), "ctx", 2, 2, 0
    )
    owner_weights = softmax_rows(blocks(query_at), blocks(keys_at), allowed, 0.0)
    owner_low = owner_weights.astype(jnp.bfloat16)
    owner_output = weighted_values(owner_low, blocks(values_at))
    owner_qgrad, owner_kgrad, owner_vgrad, unused = attention_grads(
        owner_weights,
        owner_low,
        blocks(query_at),
        blocks(keys_at),
        blocks(values_at),
        blocks(cot_at),
    )
    output_home, query_grad_home, keys_grad_home, values_grad_home = sent_together(
        (
            unblock(owner_output),
            unblock(owner_qgrad.astype(jnp.bfloat16)),
            unblock(owner_kgrad.astype(jnp.bfloat16)),
            unblock(owner_vgrad.astype(jnp.bfloat16)),
        ),
        "ctx",
        2,
        2,
        0,
    )
    key_sums = jnp.sum(blocks(keys_at), axis=1, dtype=jnp.float32)
    centroids = key_sums / jnp.sqrt(jnp.mean(key_sums * key_sums, axis=-1, keepdims=True) + EPSILON)
    centroids = centroids.reshape(heads_here, per_dev, head_dim)
    return (
        unpack(output_home),
        unpack(query_grad_home),
        unpack(keys_grad_home),
        unpack(values_grad_home),
        centroids,
        merge_local(local_output),
        merge_local(local_qgrad),
        merge_local(own_keys),
        merge_local(own_values),
        bias_grad,
    )


def solution(mesh):
    return jax.shard_map(
        shards,
        mesh=mesh,
        in_specs=(
            P("ctx", "head"),
            P("ctx", "head"),
            P("ctx", "head"),
            P("ctx", "head"),
            P("ctx", "head"),
            P("ctx", "head"),
            P("ctx", "head"),
            P("ctx", "head"),
            P("head", "ctx"),
            P("head", None),
            P(),
        ),
        out_specs=(
            P("ctx", "head"),
            P("ctx", "head"),
            P("ctx", "head"),
            P("ctx", "head"),
            P("head", "ctx", None),
            P("ctx", "head"),
            P("ctx", "head"),
            P("ctx", "head"),
            P("ctx", "head"),
            P(),
        ),
        check_vma=False,
    )
```

profile of v0, /device:TPU:0, one launch (start us, length us, event | category | flops | bytes accessed | tf_op | source)
XLA Modules:
  0.0 587.6 jit_solution(2514538544892649911)
XLA Ops:
  9.2 1.0 scatter_custom_fusion.1
  10.2 0.7 reshape.658
  10.9 7.1 %all-to-all-start = ((s32[1,16,8]{2,0,1:T(1,128)}), s32[1,16,8]{2,0,1:T(1,128)S(1)}, u32[]{:S(2)}, u32[]{:S(2)}) async-start(s32[1,16,8]{2,0,1:T(1,128)} %bitcast.4), calls=%async_computation | async-start | bytes 16384 | tf_op jit(solution)/shard_map/all_to_all | solution.py:164
  18.0 0.8 slice.100
  18.7 3.8 collective-permute-start.1
  22.6 0.8 slice.97
  23.3 3.4 collective-permute-start
  27.9 0.6 copy-done.1
  28.5 193.9 %gather_fusion = f32[32768]{0:T(1024)S(1)} fusion(f32[128]{0:T(128)S(1)} %copy-done.1, s32[32768]{0:T(1024)S(1)} %broadcast_clamp_fusion), kind=kCustom, calls=%fused_computation | custom fusion | bytes 393216 | tf_op jit(solution)/shard_map/jit(_take)/gather | solution.py:193
  223.2 0.7 fusion.72
  223.9 3.5 gather_fusion.1
  227.5 3.5 gather_fusion.2
  231.0 3.5 gather_fusion.3
  234.5 2.4 scatter_custom_fusion.2
  237.0 2.2 scatter_custom_fusion.6
  239.2 2.2 scatter_custom_fusion.5
  241.4 2.2 scatter_custom_fusion.4
  243.6 2.2 scatter_custom_fusion.3
  245.9 1.3 copy.128
  247.2 6.3 %all-to-all-start.1 = ((bf16[4,8,16,8,128]{4,3,1,0,2:T(8,128)(2,1)}), bf16[4,8,16,8,128]{4,3,1,0,2:T(8,128)(2,1)S(1)}, u32[]{:S(2)}, u32[]{:S(2)}) async-start(bf16[4,8,16,8,128]{4,3,1,0,2:T(8,128)(2,1)} %copy.128), calls=%async_computation.1 | async-start | bytes 2097152 | tf_op jit(solution)/shard_map/all_to_all | solution.py:34
  253.6 0.9 copy-done.7
  256.5 226.3 %scatter_custom_fusion = f32[129]{0:T(256)S(1)} fusion(s32[32768]{0:T(1024)S(1)} %bitcast.221, f32[32768]{0:T(1024)S(1)} %bitcast.222, f32[]{:T(128)} %constant.135.clone.1), kind=kCustom, calls=%fused_computation.165 | custom fusion | flops 32768 | bytes 520 | tf_op jit(solution)/shard_map/scatter-add | solution.py:242
  482.8 33.1 %all-gather.1 = f32[128,1,128]{2,1,0:T(1,128)S(1)} all-gather(f32[1,1,128]{2,1,0:T(1,128)S(1)} %slice_bitcast_fusion), channel_id=2, replica_groups=mesh['ctx'=16,'head'=8] {'ctx','head'}, dimensions={0}, use_global_device_ids=true | all-gather | bytes 66048 | tf_op jit(solution)/shard_map/all_gather | solution.py:22
  515.9 0.7 reduce_sum.95
  516.6 0.6 fusion.68
  517.3 1.3 collective-permute-start.3
  518.8 0.6 fusion.69
  519.4 1.3 collective-permute-start.2
  520.7 0.7 fusion.19
  521.4 0.7 fusion.17
  522.1 1.3 convolution_convert_fusion.2
  523.3 0.9 fusion.15
  524.3 0.9 fusion.95
  526.3 1.5 fusion.14
  527.9 2.3 fusion.13
  530.2 1.3 multiply_reduce_fusion.1
  532.6 0.8 copy-done.5
  533.5 1.3 copy.112
  534.8 8.6 %all-to-all-start.2 = ((bf16[4,8,16,8,128]{4,3,1,0,2:T(8,128)(2,1)}), bf16[4,8,16,8,128]{4,3,1,0,2:T(8,128)(2,1)S(1)}, u32[]{:S(2)}, u32[]{:S(2)}) async-start(bf16[4,8,16,8,128]{4,3,1,0,2:T(8,128)(2,1)} %copy.112), calls=%async_computation.2 | async-start | bytes 2097152 | tf_op jit(solution)/shard_map/all_to_all | solution.py:34
  543.5 0.8 fusion.67
  544.4 0.8 fusion.63
  545.2 0.6 copy-done.9
  545.9 0.7 bitcast_divide_fusion
  546.6 14.4 %all-to-all-done.2 = bf16[4,8,16,8,128]{4,3,1,0,2:T(8,128)(2,1)S(1)} async-done(((bf16[4,8,16,8,128]{4,3,1,0,2:T(8,128)(2,1)}), bf16[4,8,16,8,128]{4,3,1,0,2:T(8,128)(2,1)S(1)}, u32[]{:S(2)}, u32[]{:S(2)}) %all-to-all-start.2) | async-done | bytes 1048608 | tf_op jit(solution)/shard_map/all_to_all | solution.py:34
  561.2 4.9 gather_fusion.7
  566.1 4.8 gather_fusion.6
  571.0 4.9 gather_fusion.5
  575.9 4.9 gather_fusion.4
  (99 shorter events, 9.2 us)
Async XLA Ops:
  7.2 247.3 %copy-start = (bf16[512,128]{1,0:T(8,128)(2,1)S(1)}, bf16[512,128]{1,0:T(8,128)(2,1)}, u32[]{:S(2)}) copy-start(bf16[512,128]{1,0:T(8,128)(2,1)} %param.19) | copy-start | bytes 393220
  7.2 216.0 %sort.19.cloned.1.call-start = ((), (), s32[]{:S(2)}) async-start(), calls=%async_computation.3 | async-start | bytes 12320 | tf_op jit(solution)/shard_map/vmap(jit(argsort))/sort | solution.py:89
  7.8 0.7 copy-start.3
  8.5 0.7 copy-start.2
  10.9 212.0 %all-to-all-start = ((s32[1,16,8]{2,0,1:T(1,128)}), s32[1,16,8]{2,0,1:T(1,128)S(1)}, u32[]{:S(2)}, u32[]{:S(2)}) async-start(s32[1,16,8]{2,0,1:T(1,128)} %bitcast.4), calls=%async_computation | async-start | bytes 16384 | tf_op jit(solution)/shard_map/all_to_all | solution.py:164
  18.7 234.8 %collective-permute-start.1 = (bf16[128,128]{1,0:T(8,128)(2,1)S(1)}, bf16[128,128]{1,0:T(8,128)(2,1)S(1)}, u32[]{:S(2)}, u32[]{:S(2)}) collective-permute-start(bf16[128,128]{1,0:T(8,128)(2,1)S(1)} %slice.100), channel_id=1, source_target_pairs={{0,8},{8,16},{16,24},{24,32},{32,40},{40,48},{48,56},{56,64},{64,7... | collective-permute-start | bytes 98312 | tf_op jit(solution)/shard_map/ppermute | solution.py:18
  23.3 230.2 %collective-permute-start = (bf16[128,128]{1,0:T(8,128)(2,1)S(1)}, bf16[128,128]{1,0:T(8,128)(2,1)S(1)}, u32[]{:S(2)}, u32[]{:S(2)}) collective-permute-start(bf16[128,128]{1,0:T(8,128)(2,1)S(1)} %slice.97), channel_id=1, source_target_pairs={{0,8},{8,16},{16,24},{24,32},{32,40},{40,48},{48,56},{56,64},{64,7... | collective-permute-start | bytes 98312 | tf_op jit(solution)/shard_map/ppermute | solution.py:18
  27.8 0.7 copy-start.1
  247.2 6.3 %copy-start.6 = (bf16[512,128]{1,0:T(8,128)(2,1)S(1)}, bf16[512,128]{1,0:T(8,128)(2,1)}, u32[]{:S(2)}) copy-start(bf16[512,128]{1,0:T(8,128)(2,1)} %param.20) | copy-start | bytes 393220
  247.2 277.1 %all-to-all-start.1 = ((bf16[4,8,16,8,128]{4,3,1,0,2:T(8,128)(2,1)}), bf16[4,8,16,8,128]{4,3,1,0,2:T(8,128)(2,1)S(1)}, u32[]{:S(2)}, u32[]{:S(2)}) async-start(bf16[4,8,16,8,128]{4,3,1,0,2:T(8,128)(2,1)} %copy.128), calls=%async_computation.1 | async-start | bytes 2097152 | tf_op jit(solution)/shard_map/all_to_all | solution.py:34
  253.5 0.9 copy-start.7
  254.5 0.9 copy-start.12
  517.3 26.2 %collective-permute-start.3 = (bf16[1,128,128]{2,1,0:T(8,128)(2,1)}, bf16[1,128,128]{2,1,0:T(8,128)(2,1)}, u32[]{:S(2)}, u32[]{:S(2)}) collective-permute-start(bf16[1,128,128]{2,1,0:T(8,128)(2,1)} %fusion.68), channel_id=1, source_target_pairs={{8,0},{16,8},{24,16},{32,24},{40,32},{48,40},{56,48},{64,56},{72,6... | collective-permute-start | bytes 98312 | tf_op jit(solution)/shard_map/ppermute | solution.py:18
  519.4 24.9 %collective-permute-start.2 = (bf16[1,128,128]{2,1,0:T(8,128)(2,1)}, bf16[1,128,128]{2,1,0:T(8,128)(2,1)}, u32[]{:S(2)}, u32[]{:S(2)}) collective-permute-start(bf16[1,128,128]{2,1,0:T(8,128)(2,1)} %fusion.69), channel_id=1, source_target_pairs={{8,0},{16,8},{24,16},{32,24},{40,32},{48,40},{56,48},{64,56},{72,6... | collective-permute-start | bytes 98312 | tf_op jit(solution)/shard_map/ppermute | solution.py:18
  525.5 0.8 copy-start.4
  532.4 1.0 copy-start.5
  534.8 8.7 %copy-start.10 = (bf16[512,128]{1,0:T(8,128)(2,1)S(1)}, bf16[512,128]{1,0:T(8,128)(2,1)}, u32[]{:S(2)}) copy-start(bf16[512,128]{1,0:T(8,128)(2,1)} %fusion.19) | copy-start | bytes 393220
  534.8 26.2 %all-to-all-start.2 = ((bf16[4,8,16,8,128]{4,3,1,0,2:T(8,128)(2,1)}), bf16[4,8,16,8,128]{4,3,1,0,2:T(8,128)(2,1)S(1)}, u32[]{:S(2)}, u32[]{:S(2)}) async-start(bf16[4,8,16,8,128]{4,3,1,0,2:T(8,128)(2,1)} %copy.112), calls=%async_computation.2 | async-start | bytes 2097152 | tf_op jit(solution)/shard_map/all_to_all | solution.py:34
  543.5 0.9 copy-start.8
  544.3 0.8 copy-start.11
  545.1 0.7 copy-start.9
Sparse Core Ops, SparseCore 0:
  11.0 2.7 sort.21.cloned.1.call-done
  (1 shorter events, 0.0 us)
where the time goes:
time: 589 us; the launch traced here: 588 us
  local copies, waits for them, and re-layouts  249 us (42%)
  other arithmetic  235 us (40%)
  blocking collectives  33.1 us (6%)
  starting transfers between devices  31.8 us (5%)
  between operations  14.7 us (2%)
  waiting for transfers between devices  14.4 us (2%)
  matrix products  9.71 us (2%)
    scatter-add x1, other arithmetic, shards(): jax.ops.segment_sum(score_total.reshape(-1), segment_ids, num_segments=WI...  226 us
    gather x2, local copies, waits for them, and re-layouts, shards(): offset_bias = jnp.take(rel_bias, jnp.clip(offset, 0, WINDOW - 1))  194 us
    all_gather x1, blocking collectives, over_pieces(): blocks = lax.all_gather(value, axis)  33.1 us
    gather x4, local copies, waits for them, and re-layouts, unpack(): rows_head[where_to]  19.4 us
    all_to_all x2, starting transfers between devices, sent_together(): lax.all_to_all(both, axis, split_axis=split_dim, concat_axis=concat_dim,...  14.9 us
    all_to_all x2, waiting for transfers between devices, sent_together(): lax.all_to_all(both, axis, split_axis=split_dim, concat_axis=concat_dim,...  14.4 us
  transfers between devices with their start and end apart: 7, of which 1 were waited for; matrix products, arithmetic and copies ran while one was open for 79% of the time, Pallas kernels for 0%

commit v1 on v0

v1 whole, which is shorter than its diff:
```python
import functools

import jax
import jax.numpy as jnp
from jax import lax
from jax.experimental import pallas as pl
from jax.experimental.pallas import tpu as pltpu
from jax.sharding import PartitionSpec as P

TOK = 512
DIM = 128
WINDOW = 128
N_CTX = 16
N_HEAD = 8
CHUNKS = 4
ROWS = 16
SPAN = N_CTX * ROWS
NEG = -1e30
EPSILON = 1e-06
SCALE = DIM ** (-0.5)
F32 = jnp.float32
BF16 = jnp.bfloat16
I32 = jnp.int32
MESH = pl.DeviceIdType.MESH


def iota(shape, dim):
    return lax.broadcasted_iota(I32, shape, dim)


def mm(a, b):
    return jnp.dot(a, b, preferred_element_type=F32)


def mm_nt(a, b):
    return lax.dot_general(a, b, (((1,), (1,)), ((), ())), preferred_element_type=F32)


def mm_tn(a, b):
    return lax.dot_general(a, b, (((0,), (0,)), ((), ())), preferred_element_type=F32)


def attention(q, k, v, g, mask):
    scores = mm_nt(q, k) * SCALE + mask
    top = jnp.max(scores, axis=-1, keepdims=True)
    e = jnp.exp(scores - top)
    p = e / jnp.sum(e, axis=-1, keepdims=True)
    p_low = p.astype(BF16)
    dp = mm_nt(g, v)
    ds = p * (dp - jnp.sum(p * dp, axis=-1, keepdims=True))
    ds_low = ds.astype(BF16)
    out = mm(p_low, v)
    dq = mm(ds_low, k) * SCALE
    dk = mm_tn(ds_low, q) * SCALE
    dv = mm_tn(p_low, g)
    return out, dq, dk, dv, ds


def kernel(
    rq, rk, rv, rg, lq, lk, lv, lg, cl, slot, rb,
    o_ro, o_rdq, o_rdk, o_rdv, o_cent, o_lo, o_ldq, o_ldk, o_ldv, o_bias,
    tok, wq, wk, wv, wg, cl_v, slot_v, rb_v,
    send, recv, ret_send, ret_recv, halo, grad_send, grad_recv,
    cnt_send, cnt_recv, bias_a, bias_a_recv, bias_b, bias_b_recv,
    flat_v, back_hot, live_v, mask_v, wbias, acc, wacc,
    ro_v, wo_v, cent_v, bias_v, bias_sum,
    in_sem, out_sem, send_sem, recv_sem, rsend_sem, rrecv_sem,
    halo_ssem, halo_rsem, grad_ssem, grad_rsem, small_ssem, small_rsem, self_sem,
):
    me = lax.axis_index("ctx")
    my_head = lax.axis_index("head")
    my_x = lax.rem(me, 4)
    my_y = lax.div(me, 4)
    ahead = lax.rem(me + 1, N_CTX)
    behind = lax.rem(me + N_CTX - 1, N_CTX)

    def peer(step):
        px = lax.rem(my_x + lax.rem(step, 4), 4)
        py = lax.rem(my_y + lax.div(step, 4), 4)
        return py * 4 + px

    def fetch(src, dst, i):
        copy = pltpu.make_async_copy(src, dst, in_sem.at[i])
        copy.start()
        return copy

    small_in = [fetch(cl, cl_v, 0), fetch(slot, slot_v, 1), fetch(rb, rb_v, 2)]
    routed_in = [
        fetch(src, tok.at[:, pl.ds(i * DIM, DIM)], 3 + i) for i, src in enumerate((rq, rk, rv, rg))
    ]
    local_in = [fetch(src, dst, 7 + i) for i, (src, dst) in enumerate(((lk, wk), (lv, wv), (lq, wq), (lg, wg)))]

    barrier = pltpu.get_barrier_semaphore()

    @pl.loop(1, N_CTX)
    def _(step):
        pl.semaphore_signal(barrier, inc=1, device_id={"ctx": peer(step)}, device_id_type=MESH)

    @pl.loop(1, N_HEAD)
    def _(step):
        pl.semaphore_signal(
            barrier, inc=1, device_id={"head": lax.rem(my_head + step, N_HEAD)}, device_id_type=MESH
        )

    for copy in small_in:
        copy.wait()
    cluster_rows = iota((DIM, TOK), 0)
    named = (cl_v[...] == cluster_rows).astype(F32).astype(BF16)
    slots16 = jnp.broadcast_to(slot_v[...].astype(F32), (16, DIM)).astype(BF16)
    slot_of = mm(slots16, named)[0:1].astype(I32)
    in_slot = slot_of == cluster_rows
    placed = in_slot.astype(F32).astype(BF16)
    upto = (iota((TOK, TOK), 0) <= iota((TOK, TOK), 1)).astype(F32).astype(BF16)
    ranks = mm(placed, upto)
    rank = jnp.sum(jnp.where(in_slot, ranks, 0.0), axis=0, keepdims=True).astype(I32) - 1
    flat = (
        ((slot_of >> 1) & 3) * SPAN + (slot_of >> 3) * ROWS + (slot_of & 1) * 8 + rank
    )
    flat_v[...] = flat
    cnt_send[...] = mm_nt(jnp.ones((16, TOK), BF16), placed)[0:1]

    for copy in routed_in:
        copy.wait()

    def pack(c):
        hot = (flat_v[...] == iota((SPAN, TOK), 0) + c * SPAN).astype(F32).astype(BF16)
        rows = mm(hot, tok[...]).astype(BF16)
        for a in range(4):
            send[c, :, a] = rows[:, a * DIM : (a + 1) * DIM].reshape(N_CTX, ROWS, DIM)

    pl.semaphore_wait(barrier, N_CTX - 1 + N_HEAD - 1)

    for copy in local_in[:2]:
        copy.wait()
    for i, src in enumerate((wk, wv)):
        pltpu.make_async_remote_copy(
            src.at[pl.ds(TOK - WINDOW, WINDOW)], halo.at[i], halo_ssem.at[i], halo_rsem.at[i],
            device_id={"ctx": ahead}, device_id_type=MESH,
        ).start()

    @pl.loop(1, N_CTX)
    def _(step):
        pltpu.make_async_remote_copy(
            cnt_send, cnt_recv.at[me], small_ssem.at[0], small_rsem.at[0],
            device_id={"ctx": peer(step)}, device_id_type=MESH,
        ).start()

    own_count = pltpu.make_async_copy(cnt_send, cnt_recv.at[me], self_sem.at[0])
    own_count.start()

    @pl.loop(0, CHUNKS)
    def _(c):
        pack(c)

        @pl.loop(1, N_CTX)
        def _(step):
            to = peer(step)
            pltpu.make_async_remote_copy(
                send.at[c, to], recv.at[c, me], send_sem.at[c], recv_sem.at[c],
                device_id={"ctx": to}, device_id_type=MESH,
            ).start()

        pltpu.make_async_copy(send.at[c, me], recv.at[c, me], recv_sem.at[c]).start()

    back_hot[...] = jnp.zeros_like(back_hot)
    flat_col = jnp.transpose(jnp.broadcast_to(flat.astype(F32), (8, TOK)))[:, 0:1].astype(I32)

    @pl.loop(0, CHUNKS)
    def _(c):
        back_hot[c] = (flat_col == iota((TOK, SPAN), 1) + c * SPAN).astype(F32).astype(BF16)

    row_i = iota((WINDOW, 2 * WINDOW), 0)
    col_i = iota((WINDOW, 2 * WINDOW), 1)
    bias_col = jnp.sum(
        jnp.where(iota((DIM, DIM), 0) == iota((DIM, DIM), 1), rb_v[...], 0.0), axis=1, keepdims=True
    )
    spread = jnp.sum(jnp.where(row_i == WINDOW - col_i, bias_col, 0.0), axis=0, keepdims=True)
    spread = jnp.broadcast_to(spread, (WINDOW, 2 * WINDOW))
    for b in range(7):
        spread = jnp.where((row_i >> b) & 1 == 1, pltpu.roll(spread, 1 << b, 1), spread)
    offset = WINDOW + row_i - col_i
    wbias[...] = jnp.where((offset >= 0) & (offset < WINDOW), spread, NEG)

    for copy in local_in[2:]:
        copy.wait()

    def local_block(b, k, v, mask):
        rows = pl.ds(b * WINDOW, WINDOW)
        out, dq, dk, dv, ds = attention(wq[rows], k, v, wg[rows], mask)
        wo_v[0, rows] = out.astype(BF16)
        wo_v[1, rows] = dq.astype(BF16)
        return dk, dv, ds

    wacc[...] = jnp.zeros_like(wacc)
    bias_v[...] = jnp.zeros_like(bias_v)

    @pl.loop(1, 4)
    def _(b):
        at = pl.multiple_of((b - 1) * WINDOW, WINDOW)
        frame = pl.ds(at, 2 * WINDOW)
        dk, dv, ds = local_block(b, wk[frame], wv[frame], wbias[...])
        wacc[0, frame] += dk
        wacc[1, frame] += dv
        bias_v[...] += ds

    for i in range(2):
        pltpu.make_async_remote_copy(
            wk.at[pl.ds(0, WINDOW)], halo.at[i], halo_ssem.at[i], halo_rsem.at[i],
            device_id={"ctx": ahead}, device_id_type=MESH,
        ).wait_recv()
    first = jnp.where((col_i < WINDOW) & (me == 0), NEG, wbias[...])
    own = pl.ds(0, WINDOW)
    dk, dv, ds = local_block(
        0,
        jnp.concatenate([halo[0], wk[own]], axis=0),
        jnp.concatenate([halo[1], wv[own]], axis=0),
        first,
    )
    for i, d in enumerate((dk, dv)):
        grad_send[i] = d[:WINDOW].astype(BF16)
        wacc[i, own] += d[WINDOW:]
        pltpu.make_async_remote_copy(
            grad_send.at[i], grad_recv.at[i], grad_ssem.at[i], grad_rsem.at[i],
            device_id={"ctx": behind}, device_id_type=MESH,
        ).start()

    total = bias_v[...] + ds
    for b in range(7):
        total = jnp.where((row_i >> b) & 1 == 1, pltpu.roll(total, 2 * WINDOW - (1 << b), 1), total)
    by_col = jnp.sum(total, axis=0, keepdims=True)
    square = (2 * WINDOW, 2 * WINDOW)
    by_row = jnp.sum(jnp.where(iota(square, 0) == iota(square, 1), by_col, 0.0), axis=1, keepdims=True)
    tall = (2 * WINDOW, WINDOW)
    bias_a[...] = jnp.sum(
        jnp.where(iota(tall, 0) == WINDOW - iota(tall, 1), by_row, 0.0), axis=0, keepdims=True
    )

    @pl.loop(1, N_CTX)
    def _(step):
        pltpu.make_async_remote_copy(
            bias_a, bias_a_recv.at[me], small_ssem.at[1], small_rsem.at[1],
            device_id={"ctx": peer(step)}, device_id_type=MESH,
        ).start()

    own_bias = pltpu.make_async_copy(bias_a, bias_a_recv.at[me], self_sem.at[1])
    own_bias.start()

    own_count.wait()
    pltpu.make_async_copy(
        cnt_recv.at[pl.ds(0, N_CTX - 1)], cnt_recv.at[pl.ds(0, N_CTX - 1)], small_rsem.at[0]
    ).wait()
    counts = jnp.concatenate([cnt_recv[s] for s in range(N_CTX)], axis=0).astype(BF16)
    wide = (DIM, CHUNKS * SPAN)
    j = iota(wide, 1)
    pick = iota(wide, 0) == me * 8 + (j >> 8) * 2 + ((j >> 3) & 1)
    picked = mm(counts, pick.astype(F32).astype(BF16))
    j = iota((N_CTX, CHUNKS * SPAN), 1)
    held = jnp.sum(
        jnp.where(iota((N_CTX, CHUNKS * SPAN), 0) == ((j >> 4) & 15), picked, 0.0), axis=0, keepdims=True
    )
    live = jnp.where((iota((1, CHUNKS * SPAN), 1) & 7).astype(F32) < held, 0.0, NEG)
    for c in range(CHUNKS):
        live_v[c] = live[:, c * SPAN : (c + 1) * SPAN]
    span = (SPAN, SPAN)
    si, sj = iota(span, 0), iota(span, 1)
    mask_v[...] = jnp.where((((si ^ sj) & 8) == 0) & (sj <= si), 0.0, NEG)

    @pl.loop(0, CHUNKS)
    def _(c):
        pltpu.make_async_copy(recv.at[c], recv.at[c], recv_sem.at[c]).wait()
        q, k, v, g = (recv[c, :, a].reshape(SPAN, DIM) for a in range(4))
        out, dq, dk, dv, _ = attention(q, k, v, g, mask_v[...] + live_v[c])
        for a, r in enumerate((out, dq, dk, dv)):
            ret_send[c, :, a] = r.astype(BF16).reshape(N_CTX, ROWS, DIM)

        @pl.loop(1, N_CTX)
        def _(step):
            to = peer(step)
            pltpu.make_async_remote_copy(
                ret_send.at[c, to], ret_recv.at[c, me], rsend_sem.at[c], rrecv_sem.at[c],
                device_id={"ctx": to}, device_id_type=MESH,
            ).start()

        pltpu.make_async_copy(ret_send.at[c, me], ret_recv.at[c, me], rrecv_sem.at[c]).start()
        pick = (((iota((16, SPAN), 1) >> 3) & 1) == iota((16, SPAN), 0)).astype(F32).astype(BF16)
        sums = mm(pick, k)[0:2]
        cent_v[c] = sums / jnp.sqrt(jnp.mean(sums * sums, axis=-1, keepdims=True) + EPSILON)

    own_bias.wait()
    pltpu.make_async_copy(
        bias_a_recv.at[pl.ds(0, N_CTX - 1)], bias_a_recv.at[pl.ds(0, N_CTX - 1)], small_rsem.at[1]
    ).wait()
    bias_b[...] = jnp.sum(bias_a_recv[...], axis=0)

    @pl.loop(1, N_HEAD)
    def _(step):
        pltpu.make_async_remote_copy(
            bias_b, bias_b_recv.at[my_head], small_ssem.at[2], small_rsem.at[2],
            device_id={"head": lax.rem(my_head + step, N_HEAD)}, device_id_type=MESH,
        ).start()

    own_sum = pltpu.make_async_copy(bias_b, bias_b_recv.at[my_head], self_sem.at[2])
    own_sum.start()

    for i in range(2):
        pltpu.make_async_remote_copy(
            grad_send.at[i], grad_recv.at[i], grad_ssem.at[i], grad_rsem.at[i],
            device_id={"ctx": behind}, device_id_type=MESH,
        ).wait_recv()
        wacc[i, pl.ds(TOK - WINDOW, WINDOW)] += grad_recv[i].astype(F32)
        wo_v[2 + i] = wacc[i].astype(BF16)
    outs = []

    def put(src, dst, i):
        copy = pltpu.make_async_copy(src, dst, out_sem.at[i])
        copy.start()
        outs.append(copy)

    for i, dst in enumerate((o_lo, o_ldq, o_ldk, o_ldv)):
        put(wo_v.at[i], dst, i)
    for c in range(CHUNKS):
        put(cent_v.at[c], o_cent.at[pl.ds(2 * c, 2)], 4 + c)

    own_sum.wait()
    pltpu.make_async_copy(
        bias_b_recv.at[pl.ds(0, N_HEAD - 1)], bias_b_recv.at[pl.ds(0, N_HEAD - 1)], small_rsem.at[2]
    ).wait()
    bias_sum[...] = jnp.sum(bias_b_recv[...], axis=0)
    put(bias_sum, o_bias, 8)

    acc[...] = jnp.zeros_like(acc)

    @pl.loop(0, CHUNKS)
    def _(c):
        pltpu.make_async_copy(ret_recv.at[c], ret_recv.at[c], rrecv_sem.at[c]).wait()
        rows = jnp.concatenate([ret_recv[c, :, a].reshape(SPAN, DIM) for a in range(4)], axis=1)
        acc[...] += mm(back_hot[c], rows)

    for a, dst in enumerate((o_ro, o_rdq, o_rdk, o_rdv)):
        ro_v[a] = acc[:, a * DIM : (a + 1) * DIM].astype(BF16)
        put(ro_v.at[a], dst, 9 + a)

    for c in range(CHUNKS):
        part = send.at[c, pl.ds(0, N_CTX - 1)]
        pltpu.make_async_copy(part, part, send_sem.at[c]).wait()
        part = ret_send.at[c, pl.ds(0, N_CTX - 1)]
        pltpu.make_async_copy(part, part, rsend_sem.at[c]).wait()
    for i in range(2):
        pltpu.make_async_copy(halo.at[i], halo.at[i], halo_ssem.at[i]).wait()
        pltpu.make_async_copy(grad_send.at[i], grad_send.at[i], grad_ssem.at[i]).wait()
    for i, n in enumerate((N_CTX, N_CTX, N_HEAD)):
        part = cnt_recv.at[pl.ds(0, n - 1)]
        pltpu.make_async_copy(part, part, small_ssem.at[i]).wait()
    for copy in outs:
        copy.wait()


def shards(rq, rk, rv, rg, lq, lk, lv, lg, clusters, cluster_slot, rel_bias):
    token_out = jax.ShapeDtypeStruct((TOK, DIM), BF16)
    vm = pltpu.VMEM
    dma = pltpu.SemaphoreType.DMA
    scratch = [
        vm((TOK, 4 * DIM), BF16),
        vm((TOK, DIM), BF16), vm((TOK, DIM), BF16), vm((TOK, DIM), BF16), vm((TOK, DIM), BF16),
        vm((1, TOK), I32), vm((1, DIM), I32), vm((1, DIM), F32),
        vm((CHUNKS, N_CTX, 4, ROWS, DIM), BF16), vm((CHUNKS, N_CTX, 4, ROWS, DIM), BF16),
        vm((CHUNKS, N_CTX, 4, ROWS, DIM), BF16), vm((CHUNKS, N_CTX, 4, ROWS, DIM), BF16),
        vm((2, WINDOW, DIM), BF16), vm((2, WINDOW, DIM), BF16), vm((2, WINDOW, DIM), BF16),
        vm((1, DIM), F32), vm((N_CTX, 1, DIM), F32),
        vm((1, DIM), F32), vm((N_CTX, 1, DIM), F32),
        vm((1, DIM), F32), vm((N_HEAD, 1, DIM), F32),
        vm((1, TOK), I32), vm((CHUNKS, TOK, SPAN), BF16), vm((CHUNKS, 1, SPAN), F32),
        vm((SPAN, SPAN), F32), vm((WINDOW, 2 * WINDOW), F32), vm((TOK, 4 * DIM), F32),
        vm((2, TOK, DIM), F32),
        vm((4, TOK, DIM), BF16), vm((4, TOK, DIM), BF16), vm((CHUNKS, 2, DIM), F32),
        vm((WINDOW, 2 * WINDOW), F32), vm((1, DIM), F32),
        dma((11,)), dma((13,)),
        dma((CHUNKS,)), dma((CHUNKS,)), dma((CHUNKS,)), dma((CHUNKS,)),
        dma((2,)), dma((2,)), dma((2,)), dma((2,)), dma((3,)), dma((3,)), dma((3,)),
    ]
    anywhere = pl.BlockSpec(memory_space=pl.ANY)
    outs = pl.pallas_call(
        kernel,
        out_shape=[token_out] * 4
        + [jax.ShapeDtypeStruct((8, DIM), F32)]
        + [token_out] * 4
        + [jax.ShapeDtypeStruct((1, DIM), F32)],
        in_specs=[anywhere] * 11,
        out_specs=[anywhere] * 10,
        scratch_shapes=scratch,
        compiler_params=pltpu.CompilerParams(
            collective_id=0, has_side_effects=True, vmem_limit_bytes=40 * 1024 * 1024
        ),
        name="routing",
    )(rq, rk, rv, rg, lq, lk, lv, lg, clusters, cluster_slot, rel_bias.reshape(1, DIM))
    ro, rdq, rdk, rdv, cent, lo, ldq, ldk, ldv, bias = outs
    return (
        ro, rdq, rdk, rdv, cent.reshape(1, 8, DIM), lo, ldq, ldk, ldv, bias.reshape(DIM),
    )


def solution(mesh):
    tokens = P("ctx", "head")
    return jax.shard_map(
        shards,
        mesh=mesh,
        in_specs=(tokens,) * 8 + (P("head", "ctx"), P("head", None), P()),
        out_specs=(tokens,) * 4 + (P("head", "ctx", None),) + (tokens,) * 4 + (P(),),
        check_vma=False,
    )
```

time: 589 us -> 53.3 us (0.09)
  other arithmetic: 235 us -> 0 us
  local copies, waits for them, and re-layouts: 249 us -> 14.9 us
  Pallas kernels: 0 us -> 37.4 us
  blocking collectives: 33.1 us -> 0 us
  starting transfers between devices: 31.8 us -> 0 us
  waiting for transfers between devices: 14.4 us -> 0 us
  between operations: 14.7 us -> 0.69 us
  matrix products: 9.71 us -> 0 us
    scatter-add x3 -> x0, other arithmetic: 228 us -> none  [the longest x1 226 us: shards(): jax.ops.segment_sum(score_total.reshape(-1), segment_ids, num_segments=WI...]
    gather x10 -> x0, local copies, waits for them, and re-layouts: 224 us -> none  [the longest x2 194 us: shards(): offset_bias = jnp.take(rel_bias, jnp.clip(offset, 0, WINDOW - 1))]
    pallas_call x0 -> x1, Pallas kernels: none -> 37.4 us  [shards(): pl.pallas_call(kernel, out_shape=[token_out] * 4 + [jax.ShapeDtypeStruct(...]
    all_gather x1 -> x0, blocking collectives: 33.1 us -> none  [over_pieces(): blocks = lax.all_gather(value, axis)]
    all_to_all x3 -> x0, starting transfers between devices: 22.1 us -> none  [the longest x2 14.9 us: sent_together(): lax.all_to_all(both, axis, split_axis=split_dim, concat_axis=concat_dim,...]
    all_to_all x3 -> x0, waiting for transfers between devices: 14.4 us -> none  [the longest x2 14.4 us: sent_together(): lax.all_to_all(both, axis, split_axis=split_dim, concat_axis=concat_dim,...]
    scatter x9 -> x0, local copies, waits for them, and re-layouts: 12.1 us -> none  [the longest x5 8.71 us: one_head(): holder = jnp.zeros((per_dev * ctx_size * per_source, head_dim), token_row...]
    unnamed x31 -> x32, local copies, waits for them, and re-layouts: 5.17 us -> 14.9 us
  transfers between devices with their start and end apart: 7 -> 0, of which waited for: 1 -> 0; matrix products, arithmetic and copies ran while one was open for 79% -> 0% of each run, Pallas kernels for 0% -> 0%
where the time goes in v1:
time: 53.3 us; the launch traced here: 53 us
  Pallas kernels  37.4 us (70%)
  local copies, waits for them, and re-layouts  14.9 us (28%)
  between operations  0.69 us (1%)
    pallas_call x1, Pallas kernels, shards(): pl.pallas_call(kernel, out_shape=[token_out] * 4 + [jax.ShapeDtypeStruct(...  37.4 us
    unnamed x32, local copies, waits for them, and re-layouts  14.9 us

profile of v1, /device:TPU:0, one launch (start us, length us, event | category | flops | bytes accessed | tf_op | source)
XLA Modules:
  0.0 53.0 jit_solution(11973996303462166994)
XLA Ops:
  0.6 0.0 copy-start.10
  0.7 0.0 copy-start.9
  0.7 0.6 %copy-done.10 = f32[128]{0:T(128)S(1)} copy-done((f32[128]{0:T(128)S(1)}, f32[128]{0:T(128)}, u32[]{:S(2)}) %copy-start.10) | copy-done | bytes 536
  1.3 0.0 copy-done.9
  1.3 0.0 copy-start
  1.3 0.9 %copy-done = bf16[512,128]{1,0:T(8,128)(2,1)S(1)} copy-done((bf16[512,128]{1,0:T(8,128)(2,1)S(1)}, bf16[512,128]{1,0:T(8,128)(2,1)}, u32[]{:S(2)}) %copy-start) | copy-done | bytes 131096
  2.2 0.0 copy-start.1
  2.2 0.9 %copy-done.1 = bf16[512,128]{1,0:T(8,128)(2,1)S(1)} copy-done((bf16[512,128]{1,0:T(8,128)(2,1)S(1)}, bf16[512,128]{1,0:T(8,128)(2,1)}, u32[]{:S(2)}) %copy-start.1) | copy-done | bytes 131096
  3.1 0.0 copy-start.2
  3.1 0.9 %copy-done.2 = bf16[512,128]{1,0:T(8,128)(2,1)S(1)} copy-done((bf16[512,128]{1,0:T(8,128)(2,1)S(1)}, bf16[512,128]{1,0:T(8,128)(2,1)}, u32[]{:S(2)}) %copy-start.2) | copy-done | bytes 131096
  4.0 0.0 copy-start.3
  4.0 0.9 %copy-done.3 = bf16[512,128]{1,0:T(8,128)(2,1)S(1)} copy-done((bf16[512,128]{1,0:T(8,128)(2,1)S(1)}, bf16[512,128]{1,0:T(8,128)(2,1)}, u32[]{:S(2)}) %copy-start.3) | copy-done | bytes 131096
  4.9 0.0 copy-start.4
  4.9 0.9 %copy-done.4 = bf16[512,128]{1,0:T(8,128)(2,1)S(1)} copy-done((bf16[512,128]{1,0:T(8,128)(2,1)S(1)}, bf16[512,128]{1,0:T(8,128)(2,1)}, u32[]{:S(2)}) %copy-start.4) | copy-done | bytes 131096
  5.8 0.0 copy-start.5
  5.8 0.9 %copy-done.5 = bf16[512,128]{1,0:T(8,128)(2,1)S(1)} copy-done((bf16[512,128]{1,0:T(8,128)(2,1)S(1)}, bf16[512,128]{1,0:T(8,128)(2,1)}, u32[]{:S(2)}) %copy-start.5) | copy-done | bytes 131096
  6.7 0.0 copy-start.6
  6.7 0.9 %copy-done.6 = bf16[512,128]{1,0:T(8,128)(2,1)S(1)} copy-done((bf16[512,128]{1,0:T(8,128)(2,1)S(1)}, bf16[512,128]{1,0:T(8,128)(2,1)}, u32[]{:S(2)}) %copy-start.6) | copy-done | bytes 131096
  7.7 0.0 copy-start.7
  7.7 0.9 %copy-done.7 = bf16[512,128]{1,0:T(8,128)(2,1)S(1)} copy-done((bf16[512,128]{1,0:T(8,128)(2,1)S(1)}, bf16[512,128]{1,0:T(8,128)(2,1)}, u32[]{:S(2)}) %copy-start.7) | copy-done | bytes 131096
  8.6 0.0 copy-start.8
  8.6 0.7 %copy-done.8 = s32[1,512]{1,0:T(1,128)S(1)} copy-done((s32[1,512]{1,0:T(1,128)S(1)}, s32[1,512]{1,0:T(1,128)}, u32[]{:S(2)}) %copy-start.8) | copy-done | bytes 2072
  9.2 37.4 %routing.1 = (bf16[512,128]{1,0:T(8,128)(2,1)S(1)}, bf16[512,128]{1,0:T(8,128)(2,1)S(1)}, bf16[512,128]{1,0:T(8,128)(2,1)S(1)}, bf16[512,128]{1,0:T(8,128)(2,1)S...) custom-call(bf16[512,128]{1,0:T(8,128)(2,1)S(1)} %copy-done, ...), custom_call_target="tpu_custom_call" | custom-call | tf_op jit(solution)/shard_map/routing/pallas_call | solution.py:382
  46.6 0.7 %copy.31 = bf16[512,128]{1,0:T(8,128)(2,1)} copy(bf16[512,128]{1,0:T(8,128)(2,1)S(1)} %get-tuple-element.40) | data formatting | bytes 262144
  47.3 0.7 %copy.32 = bf16[512,128]{1,0:T(8,128)(2,1)} copy(bf16[512,128]{1,0:T(8,128)(2,1)S(1)} %get-tuple-element.41) | data formatting | bytes 262144
  48.0 0.7 %copy.33 = bf16[512,128]{1,0:T(8,128)(2,1)} copy(bf16[512,128]{1,0:T(8,128)(2,1)S(1)} %get-tuple-element.42) | data formatting | bytes 262144
  48.6 0.7 %copy.34 = bf16[512,128]{1,0:T(8,128)(2,1)} copy(bf16[512,128]{1,0:T(8,128)(2,1)S(1)} %get-tuple-element.43) | data formatting | bytes 262144
  49.3 0.6 %copy.35 = f32[1,8,128]{2,1,0:T(8,128)} copy(f32[1,8,128]{2,1,0:T(8,128)S(1)} %bitcast.3) | data formatting | bytes 8192
  49.9 0.7 %copy.36 = bf16[512,128]{1,0:T(8,128)(2,1)} copy(bf16[512,128]{1,0:T(8,128)(2,1)S(1)} %get-tuple-element.45) | data formatting | bytes 262144
  50.5 0.7 %copy.37 = bf16[512,128]{1,0:T(8,128)(2,1)} copy(bf16[512,128]{1,0:T(8,128)(2,1)S(1)} %get-tuple-element.46) | data formatting | bytes 262144
  51.2 0.7 %copy.38 = bf16[512,128]{1,0:T(8,128)(2,1)} copy(bf16[512,128]{1,0:T(8,128)(2,1)S(1)} %get-tuple-element.47) | data formatting | bytes 262144
  51.8 0.7 %copy.39 = bf16[512,128]{1,0:T(8,128)(2,1)} copy(bf16[512,128]{1,0:T(8,128)(2,1)S(1)} %get-tuple-element.48) | data formatting | bytes 262144
  52.5 0.5 copy.40
Async XLA Ops:
  0.6 0.7 %copy-start.10 = (f32[128]{0:T(128)S(1)}, f32[128]{0:T(128)}, u32[]{:S(2)}) copy-start(f32[128]{0:T(128)} %param.21) | copy-start | bytes 1540
  0.7 0.7 %copy-start.9 = (s32[1,128]{1,0:T(1,128)S(1)}, s32[1,128]{1,0:T(1,128)}, u32[]{:S(2)}) copy-start(s32[1,128]{1,0:T(1,128)} %slot.1) | copy-start | bytes 1540
  1.3 0.9 %copy-start = (bf16[512,128]{1,0:T(8,128)(2,1)S(1)}, bf16[512,128]{1,0:T(8,128)(2,1)}, u32[]{:S(2)}) copy-start(bf16[512,128]{1,0:T(8,128)(2,1)} %rq.1) | copy-start | bytes 393220
  2.2 0.9 %copy-start.1 = (bf16[512,128]{1,0:T(8,128)(2,1)S(1)}, bf16[512,128]{1,0:T(8,128)(2,1)}, u32[]{:S(2)}) copy-start(bf16[512,128]{1,0:T(8,128)(2,1)} %rk.1) | copy-start | bytes 393220
  3.1 0.9 %copy-start.2 = (bf16[512,128]{1,0:T(8,128)(2,1)S(1)}, bf16[512,128]{1,0:T(8,128)(2,1)}, u32[]{:S(2)}) copy-start(bf16[512,128]{1,0:T(8,128)(2,1)} %rv.1) | copy-start | bytes 393220
  4.0 0.9 %copy-start.3 = (bf16[512,128]{1,0:T(8,128)(2,1)S(1)}, bf16[512,128]{1,0:T(8,128)(2,1)}, u32[]{:S(2)}) copy-start(bf16[512,128]{1,0:T(8,128)(2,1)} %rg.1) | copy-start | bytes 393220
  4.9 0.9 %copy-start.4 = (bf16[512,128]{1,0:T(8,128)(2,1)S(1)}, bf16[512,128]{1,0:T(8,128)(2,1)}, u32[]{:S(2)}) copy-start(bf16[512,128]{1,0:T(8,128)(2,1)} %lq.1) | copy-start | bytes 393220
  5.8 0.9 %copy-start.5 = (bf16[512,128]{1,0:T(8,128)(2,1)S(1)}, bf16[512,128]{1,0:T(8,128)(2,1)}, u32[]{:S(2)}) copy-start(bf16[512,128]{1,0:T(8,128)(2,1)} %lk.1) | copy-start | bytes 393220
  6.7 0.9 %copy-start.6 = (bf16[512,128]{1,0:T(8,128)(2,1)S(1)}, bf16[512,128]{1,0:T(8,128)(2,1)}, u32[]{:S(2)}) copy-start(bf16[512,128]{1,0:T(8,128)(2,1)} %lv.1) | copy-start | bytes 393220
  7.7 0.9 %copy-start.7 = (bf16[512,128]{1,0:T(8,128)(2,1)S(1)}, bf16[512,128]{1,0:T(8,128)(2,1)}, u32[]{:S(2)}) copy-start(bf16[512,128]{1,0:T(8,128)(2,1)} %lg.1) | copy-start | bytes 393220
  8.6 0.7 %copy-start.8 = (s32[1,512]{1,0:T(1,128)S(1)}, s32[1,512]{1,0:T(1,128)}, u32[]{:S(2)}) copy-start(s32[1,512]{1,0:T(1,128)} %cl.1) | copy-start | bytes 6148

commit v2 on v1

--- a/solution.py
+++ b/solution.py
@@ -17,6 +17,7 @@
 SPAN = N_CTX * ROWS
 NEG = -1e30
 EPSILON = 1e-06
+VMEM_GRANT = 54140 * 1024
 SCALE = DIM ** (-0.5)
 F32 = jnp.float32
 BF16 = jnp.bfloat16
@@ -58,13 +59,13 @@
 
 def kernel(
     rq, rk, rv, rg, lq, lk, lv, lg, cl, slot, rb,
-    o_ro, o_rdq, o_rdk, o_rdv, o_cent, o_lo, o_ldq, o_ldk, o_ldv, o_bias,
-    tok, wq, wk, wv, wg, cl_v, slot_v, rb_v,
+    o_ro, o_rdq, o_rdk, o_rdv, o_lo, o_ldq, o_ldk, o_ldv, o_cent, o_bias,
+    tok, wq, wk, wv, wg,
     send, recv, ret_send, ret_recv, halo, grad_send, grad_recv,
     cnt_send, cnt_recv, bias_a, bias_a_recv, bias_b, bias_b_recv,
     flat_v, back_hot, live_v, mask_v, wbias, acc, wacc,
-    ro_v, wo_v, cent_v, bias_v, bias_sum,
-    in_sem, out_sem, send_sem, recv_sem, rsend_sem, rrecv_sem,
+    bias_v,
+    in_sem, send_sem, recv_sem, rsend_sem, rrecv_sem,
     halo_ssem, halo_rsem, grad_ssem, grad_rsem, small_ssem, small_rsem, self_sem,
 ):
     me = lax.axis_index("ctx")
@@ -84,11 +85,10 @@
         copy.start()
         return copy
 
-    small_in = [fetch(cl, cl_v, 0), fetch(slot, slot_v, 1), fetch(rb, rb_v, 2)]
     routed_in = [
-        fetch(src, tok.at[:, pl.ds(i * DIM, DIM)], 3 + i) for i, src in enumerate((rq, rk, rv, rg))
+        fetch(src, tok.at[:, pl.ds(i * DIM, DIM)], i) for i, src in enumerate((rq, rk, rv, rg))
     ]
-    local_in = [fetch(src, dst, 7 + i) for i, (src, dst) in enumerate(((lk, wk), (lv, wv), (lq, wq), (lg, wg)))]
+    local_in = [fetch(src, dst, 4 + i) for i, (src, dst) in enumerate(((lk, wk), (lv, wv), (lq, wq), (lg, wg)))]
 
     barrier = pltpu.get_barrier_semaphore()
 
@@ -102,11 +102,9 @@
             barrier, inc=1, device_id={"head": lax.rem(my_head + step, N_HEAD)}, device_id_type=MESH
         )
 
-    for copy in small_in:
-        copy.wait()
     cluster_rows = iota((DIM, TOK), 0)
-    named = (cl_v[...] == cluster_rows).astype(F32).astype(BF16)
-    slots16 = jnp.broadcast_to(slot_v[...].astype(F32), (16, DIM)).astype(BF16)
+    named = (cl[...] == cluster_rows).astype(F32).astype(BF16)
+    slots16 = jnp.broadcast_to(slot[...].astype(F32), (16, DIM)).astype(BF16)
     slot_of = mm(slots16, named)[0:1].astype(I32)
     in_slot = slot_of == cluster_rows
     placed = in_slot.astype(F32).astype(BF16)
@@ -172,7 +170,7 @@
     row_i = iota((WINDOW, 2 * WINDOW), 0)
     col_i = iota((WINDOW, 2 * WINDOW), 1)
     bias_col = jnp.sum(
-        jnp.where(iota((DIM, DIM), 0) == iota((DIM, DIM), 1), rb_v[...], 0.0), axis=1, keepdims=True
+        jnp.where(iota((DIM, DIM), 0) == iota((DIM, DIM), 1), rb[...], 0.0), axis=1, keepdims=True
     )
     spread = jnp.sum(jnp.where(row_i == WINDOW - col_i, bias_col, 0.0), axis=0, keepdims=True)
     spread = jnp.broadcast_to(spread, (WINDOW, 2 * WINDOW))
@@ -187,8 +185,8 @@
     def local_block(b, k, v, mask):
         rows = pl.ds(b * WINDOW, WINDOW)
         out, dq, dk, dv, ds = attention(wq[rows], k, v, wg[rows], mask)
-        wo_v[0, rows] = out.astype(BF16)
-        wo_v[1, rows] = dq.astype(BF16)
+        o_lo[rows] = out.astype(BF16)
+        o_ldq[rows] = dq.astype(BF16)
         return dk, dv, ds
 
     wacc[...] = jnp.zeros_like(wacc)
@@ -284,7 +282,7 @@
         pltpu.make_async_copy(ret_send.at[c, me], ret_recv.at[c, me], rrecv_sem.at[c]).start()
         pick = (((iota((16, SPAN), 1) >> 3) & 1) == iota((16, SPAN), 0)).astype(F32).astype(BF16)
         sums = mm(pick, k)[0:2]
-        cent_v[c] = sums / jnp.sqrt(jnp.mean(sums * sums, axis=-1, keepdims=True) + EPSILON)
+        o_cent[c] = sums / jnp.sqrt(jnp.mean(sums * sums, axis=-1, keepdims=True) + EPSILON)
 
     own_bias.wait()
     pltpu.make_async_copy(
@@ -308,25 +306,12 @@
             device_id={"ctx": behind}, device_id_type=MESH,
         ).wait_recv()
         wacc[i, pl.ds(TOK - WINDOW, WINDOW)] += grad_recv[i].astype(F32)
-        wo_v[2 + i] = wacc[i].astype(BF16)
-    outs = []
-
-    def put(src, dst, i):
-        copy = pltpu.make_async_copy(src, dst, out_sem.at[i])
-        copy.start()
-        outs.append(copy)
-
-    for i, dst in enumerate((o_lo, o_ldq, o_ldk, o_ldv)):
-        put(wo_v.at[i], dst, i)
-    for c in range(CHUNKS):
-        put(cent_v.at[c], o_cent.at[pl.ds(2 * c, 2)], 4 + c)
-
+        (o_ldk, o_ldv)[i][...] = wacc[i].astype(BF16)
     own_sum.wait()
     pltpu.make_async_copy(
         bias_b_recv.at[pl.ds(0, N_HEAD - 1)], bias_b_recv.at[pl.ds(0, N_HEAD - 1)], small_rsem.at[2]
     ).wait()
-    bias_sum[...] = jnp.sum(bias_b_recv[...], axis=0)
-    put(bias_sum, o_bias, 8)
+    o_bias[...] = jnp.sum(bias_b_recv[...], axis=0)
 
     acc[...] = jnp.zeros_like(acc)
 
@@ -337,8 +322,7 @@
         acc[...] += mm(back_hot[c], rows)
 
     for a, dst in enumerate((o_ro, o_rdq, o_rdk, o_rdv)):
-        ro_v[a] = acc[:, a * DIM : (a + 1) * DIM].astype(BF16)
-        put(ro_v.at[a], dst, 9 + a)
+        dst[...] = acc[:, a * DIM : (a + 1) * DIM].astype(BF16)
 
     for c in range(CHUNKS):
         part = send.at[c, pl.ds(0, N_CTX - 1)]
@@ -351,7 +335,14 @@
     for i, n in enumerate((N_CTX, N_CTX, N_HEAD)):
         part = cnt_recv.at[pl.ds(0, n - 1)]
         pltpu.make_async_copy(part, part, small_ssem.at[i]).wait()
-    for copy in outs:
+
+
+def deliver(*refs):
+    sources, targets, sems = refs[:10], refs[10:20], refs[20]
+    copies = [pltpu.make_async_copy(s, t, sems.at[i]) for i, (s, t) in enumerate(zip(sources, targets))]
+    for copy in copies:
+        copy.start()
+    for copy in copies:
         copy.wait()
 
 
@@ -362,7 +353,6 @@
     scratch = [
         vm((TOK, 4 * DIM), BF16),
         vm((TOK, DIM), BF16), vm((TOK, DIM), BF16), vm((TOK, DIM), BF16), vm((TOK, DIM), BF16),
-        vm((1, TOK), I32), vm((1, DIM), I32), vm((1, DIM), F32),
         vm((CHUNKS, N_CTX, 4, ROWS, DIM), BF16), vm((CHUNKS, N_CTX, 4, ROWS, DIM), BF16),
         vm((CHUNKS, N_CTX, 4, ROWS, DIM), BF16), vm((CHUNKS, N_CTX, 4, ROWS, DIM), BF16),
         vm((2, WINDOW, DIM), BF16), vm((2, WINDOW, DIM), BF16), vm((2, WINDOW, DIM), BF16),
@@ -372,28 +362,33 @@
         vm((1, TOK), I32), vm((CHUNKS, TOK, SPAN), BF16), vm((CHUNKS, 1, SPAN), F32),
         vm((SPAN, SPAN), F32), vm((WINDOW, 2 * WINDOW), F32), vm((TOK, 4 * DIM), F32),
         vm((2, TOK, DIM), F32),
-        vm((4, TOK, DIM), BF16), vm((4, TOK, DIM), BF16), vm((CHUNKS, 2, DIM), F32),
-        vm((WINDOW, 2 * WINDOW), F32), vm((1, DIM), F32),
-        dma((11,)), dma((13,)),
+        vm((WINDOW, 2 * WINDOW), F32),
+        dma((8,)),
         dma((CHUNKS,)), dma((CHUNKS,)), dma((CHUNKS,)), dma((CHUNKS,)),
         dma((2,)), dma((2,)), dma((2,)), dma((2,)), dma((3,)), dma((3,)), dma((3,)),
     ]
     anywhere = pl.BlockSpec(memory_space=pl.ANY)
-    outs = pl.pallas_call(
+    small = [jax.ShapeDtypeStruct((CHUNKS, 2, DIM), F32), jax.ShapeDtypeStruct((1, DIM), F32)]
+    packed = pl.pallas_call(
         kernel,
-        out_shape=[token_out] * 4
-        + [jax.ShapeDtypeStruct((8, DIM), F32)]
-        + [token_out] * 4
-        + [jax.ShapeDtypeStruct((1, DIM), F32)],
-        in_specs=[anywhere] * 11,
-        out_specs=[anywhere] * 10,
+        out_shape=[token_out] * 8 + small,
+        in_specs=[anywhere] * 8 + [pl.BlockSpec(memory_space=pltpu.VMEM)] * 3,
+        out_specs=[pl.BlockSpec(memory_space=pltpu.VMEM)] * 10,
         scratch_shapes=scratch,
         compiler_params=pltpu.CompilerParams(
-            collective_id=0, has_side_effects=True, vmem_limit_bytes=40 * 1024 * 1024
+            collective_id=0, has_side_effects=True, vmem_limit_bytes=VMEM_GRANT
         ),
         name="routing",
     )(rq, rk, rv, rg, lq, lk, lv, lg, clusters, cluster_slot, rel_bias.reshape(1, DIM))
-    ro, rdq, rdk, rdv, cent, lo, ldq, ldk, ldv, bias = outs
+    ro, rdq, rdk, rdv, lo, ldq, ldk, ldv, cent, bias = pl.pallas_call(
+        deliver,
+        out_shape=[token_out] * 8 + small,
+        in_specs=[anywhere] * 10,
+        out_specs=[anywhere] * 10,
+        scratch_shapes=[dma((10,))],
+        compiler_params=pltpu.CompilerParams(vmem_limit_bytes=VMEM_GRANT),
+        name="deliver",
+    )(*packed)
     return (
         ro, rdq, rdk, rdv, cent.reshape(1, 8, DIM), lo, ldq, ldk, ldv, bias.reshape(DIM),
     )

time: 53.3 us -> 38.7 us (0.73)
  local copies, waits for them, and re-layouts: 14.9 us -> 1.34 us
  Pallas kernels: 37.4 us -> 36.5 us
    unnamed x32 -> x6, local copies, waits for them, and re-layouts: 14.9 us -> 1.34 us
    pallas_call x1 -> x2, Pallas kernels: 37.4 us -> 36.5 us  [the longest x1 35.4 us: shards(): pl.pallas_call(kernel, out_shape=[token_out] * 8 + small, in_specs=[anywh...]
where the time goes in v2:
time: 38.7 us; the launch traced here: 38.5 us
  Pallas kernels  36.5 us (94%)
  local copies, waits for them, and re-layouts  1.34 us (3%)
  between operations  0.67 us (2%)
    pallas_call x1, Pallas kernels, shards(): pl.pallas_call(kernel, out_shape=[token_out] * 8 + small, in_specs=[anywh...  35.4 us
    unnamed x6, local copies, waits for them, and re-layouts  1.34 us
    pallas_call x1, Pallas kernels, shards(): pl.pallas_call(deliver, out_shape=[token_out] * 8 + small, in_specs=[anyw...  1.06 us

profile of v2, /device:TPU:0, one launch (start us, length us, event | category | flops | bytes accessed | tf_op | source)
XLA Modules:
  0.0 38.5 jit_solution(5233197662908094435)
XLA Ops:
  0.6 0.0 copy-start.2
  0.7 0.0 copy-start.1
  0.7 0.6 %copy-done.2 = f32[128]{0:T(128)S(1)} copy-done((f32[128]{0:T(128)S(1)}, f32[128]{0:T(128)}, u32[]{:S(2)}) %copy-start.2) | copy-done | bytes 536
  1.3 0.0 copy-done.1
  1.3 0.0 copy-start
  1.3 0.7 %copy-done = s32[1,512]{1,0:T(1,128)S(1)} copy-done((s32[1,512]{1,0:T(1,128)S(1)}, s32[1,512]{1,0:T(1,128)}, u32[]{:S(2)}) %copy-start) | copy-done | bytes 2072
  2.0 35.4 %routing.1 = (bf16[512,128]{1,0:T(8,128)(2,1)S(1)}, bf16[512,128]{1,0:T(8,128)(2,1)S(1)}, bf16[512,128]{1,0:T(8,128)(2,1)S(1)}, bf16[512,128]{1,0:T(8,128)(2,1)S...) custom-call(bf16[512,128]{1,0:T(8,128)(2,1)} %rq.1, ...), custom_call_target="tpu_custom_call" | custom-call | tf_op jit(solution)/shard_map/routing/pallas_call | solution.py:372
  37.4 1.1 %deliver.1 = (bf16[512,128]{1,0:T(8,128)(2,1)}, bf16[512,128]{1,0:T(8,128)(2,1)}, bf16[512,128]{1,0:T(8,128)(2,1)}, bf16[512,128]{1,0:T(8,128)(2,1)}, bf16[512,1...) custom-call(bf16[512,128]{1,0:T(8,128)(2,1)S(1)} %get-tuple-element., ...), custom_call_target="tpu_custom_call" | custom-call | tf_op jit(solution)/shard_map/deliver/pallas_call | solution.py:383
Async XLA Ops:
  0.6 0.7 %copy-start.2 = (f32[128]{0:T(128)S(1)}, f32[128]{0:T(128)}, u32[]{:S(2)}) copy-start(f32[128]{0:T(128)} %param.21) | copy-start | bytes 1540
  0.7 0.7 %copy-start.1 = (s32[1,128]{1,0:T(1,128)S(1)}, s32[1,128]{1,0:T(1,128)}, u32[]{:S(2)}) copy-start(s32[1,128]{1,0:T(1,128)} %slot.1) | copy-start | bytes 1540
  1.3 0.7 %copy-start = (s32[1,512]{1,0:T(1,128)S(1)}, s32[1,512]{1,0:T(1,128)}, u32[]{:S(2)}) copy-start(s32[1,512]{1,0:T(1,128)} %cl.1) | copy-start | bytes 6148

commit v3 on v2

--- a/solution.py
+++ b/solution.py
@@ -41,6 +41,10 @@
     return lax.dot_general(a, b, (((0,), (0,)), ((), ())), preferred_element_type=F32)
 
 
+def landed(part, sem):
+    pltpu.make_async_copy(part, part, sem).wait()
+
+
 def attention(q, k, v, g, mask):
     scores = mm_nt(q, k) * SCALE + mask
     top = jnp.max(scores, axis=-1, keepdims=True)
@@ -62,11 +66,11 @@
     o_ro, o_rdq, o_rdk, o_rdv, o_lo, o_ldq, o_ldk, o_ldv, o_cent, o_bias,
     tok, wq, wk, wv, wg,
     send, recv, ret_send, ret_recv, halo, grad_send, grad_recv,
-    cnt_send, cnt_recv, bias_a, bias_a_recv, bias_b, bias_b_recv,
+    cnt_send, cnt_recv, bias_a, bias_a_recv, bias_b, bias_b_recv, bias_c, bias_d,
     flat_v, back_hot, live_v, mask_v, wbias, acc, wacc,
     bias_v,
     in_sem, send_sem, recv_sem, rsend_sem, rrecv_sem,
-    halo_ssem, halo_rsem, grad_ssem, grad_rsem, small_ssem, small_rsem, self_sem,
+    halo_ssem, halo_rsem, grad_ssem, grad_rsem, small_ssem, small_rsem, go_sem,
 ):
     me = lax.axis_index("ctx")
     my_head = lax.axis_index("head")
@@ -80,6 +84,25 @@
         py = lax.rem(my_y + lax.div(step, 4), 4)
         return py * 4 + px
 
+    lead = me == 0
+    barrier = pltpu.get_barrier_semaphore()
+
+    @pl.loop(1, N_CTX)
+    def _(step):
+        to = peer(step)
+
+        @pl.when(to != 0)
+        def _():
+            pl.semaphore_signal(barrier, inc=1, device_id={"ctx": to}, device_id_type=MESH)
+
+    @pl.when(lead)
+    def _():
+        @pl.loop(1, N_HEAD)
+        def _(step):
+            pl.semaphore_signal(
+                barrier, inc=1, device_id={"head": lax.rem(my_head + step, N_HEAD)}, device_id_type=MESH
+            )
+
     def fetch(src, dst, i):
         copy = pltpu.make_async_copy(src, dst, in_sem.at[i])
         copy.start()
@@ -89,18 +112,6 @@
         fetch(src, tok.at[:, pl.ds(i * DIM, DIM)], i) for i, src in enumerate((rq, rk, rv, rg))
     ]
     local_in = [fetch(src, dst, 4 + i) for i, (src, dst) in enumerate(((lk, wk), (lv, wv), (lq, wq), (lg, wg)))]
-
-    barrier = pltpu.get_barrier_semaphore()
-
-    @pl.loop(1, N_CTX)
-    def _(step):
-        pl.semaphore_signal(barrier, inc=1, device_id={"ctx": peer(step)}, device_id_type=MESH)
-
-    @pl.loop(1, N_HEAD)
-    def _(step):
-        pl.semaphore_signal(
-            barrier, inc=1, device_id={"head": lax.rem(my_head + step, N_HEAD)}, device_id_type=MESH
-        )
 
     cluster_rows = iota((DIM, TOK), 0)
     named = (cl[...] == cluster_rows).astype(F32).astype(BF16)
@@ -126,7 +137,15 @@
         for a in range(4):
             send[c, :, a] = rows[:, a * DIM : (a + 1) * DIM].reshape(N_CTX, ROWS, DIM)
 
-    pl.semaphore_wait(barrier, N_CTX - 1 + N_HEAD - 1)
+    @pl.when(me != 0)
+    def _():
+        pl.semaphore_wait(barrier, N_CTX - 1)
+        pl.semaphore_signal(go_sem, inc=1, device_id={"ctx": 0}, device_id_type=MESH)
+
+    @pl.when(lead)
+    def _():
+        pl.semaphore_wait(go_sem, N_CTX - 1)
+
 
     for copy in local_in[:2]:
         copy.wait()
@@ -143,8 +162,7 @@
             device_id={"ctx": peer(step)}, device_id_type=MESH,
         ).start()
 
-    own_count = pltpu.make_async_copy(cnt_send, cnt_recv.at[me], self_sem.at[0])
-    own_count.start()
+    cnt_recv[me] = cnt_send[...]
 
     @pl.loop(0, CHUNKS)
     def _(c):
@@ -158,7 +176,7 @@
                 device_id={"ctx": to}, device_id_type=MESH,
             ).start()
 
-        pltpu.make_async_copy(send.at[c, me], recv.at[c, me], recv_sem.at[c]).start()
+        recv[c, me] = send[c, me]
 
     back_hot[...] = jnp.zeros_like(back_hot)
     flat_col = jnp.transpose(jnp.broadcast_to(flat.astype(F32), (8, TOK)))[:, 0:1].astype(I32)
@@ -233,20 +251,18 @@
         jnp.where(iota(tall, 0) == WINDOW - iota(tall, 1), by_row, 0.0), axis=0, keepdims=True
     )
 
-    @pl.loop(1, N_CTX)
-    def _(step):
+    @pl.when(me != 0)
+    def _():
         pltpu.make_async_remote_copy(
             bias_a, bias_a_recv.at[me], small_ssem.at[1], small_rsem.at[1],
-            device_id={"ctx": peer(step)}, device_id_type=MESH,
+            device_id={"ctx": 0}, device_id_type=MESH,
         ).start()
 
-    own_bias = pltpu.make_async_copy(bias_a, bias_a_recv.at[me], self_sem.at[1])
-    own_bias.start()
-
-    own_count.wait()
-    pltpu.make_async_copy(
-        cnt_recv.at[pl.ds(0, N_CTX - 1)], cnt_recv.at[pl.ds(0, N_CTX - 1)], small_rsem.at[0]
-    ).wait()
+    @pl.when(lead)
+    def _():
+        bias_a_recv[0] = bias_a[...]
+
+    landed(cnt_recv.at[pl.ds(0, N_CTX - 1)], small_rsem.at[0])
     counts = jnp.concatenate([cnt_recv[s] for s in range(N_CTX)], axis=0).astype(BF16)
     wide = (DIM, CHUNKS * SPAN)
     j = iota(wide, 1)
@@ -265,7 +281,21 @@
 
     @pl.loop(0, CHUNKS)
     def _(c):
-        pltpu.make_async_copy(recv.at[c], recv.at[c], recv_sem.at[c]).wait()
+        @pl.when(lead & (c == 1))
+        def _():
+            landed(bias_a_recv.at[pl.ds(0, N_CTX - 1)], small_rsem.at[1])
+            bias_b[...] = jnp.sum(bias_a_recv[...], axis=0)
+            bias_b_recv[my_head] = bias_b[...]
+            pl.semaphore_wait(barrier, N_HEAD - 1)
+
+            @pl.loop(1, N_HEAD)
+            def _(step):
+                pltpu.make_async_remote_copy(
+                    bias_b, bias_b_recv.at[my_head], small_ssem.at[2], small_rsem.at[2],
+                    device_id={"head": lax.rem(my_head + step, N_HEAD)}, device_id_type=MESH,
+                ).start()
+
+        landed(recv.at[c, pl.ds(0, N_CTX - 1)], recv_sem.at[c])
         q, k, v, g = (recv[c, :, a].reshape(SPAN, DIM) for a in range(4))
         out, dq, dk, dv, _ = attention(q, k, v, g, mask_v[...] + live_v[c])
         for a, r in enumerate((out, dq, dk, dv)):
@@ -279,26 +309,22 @@
                 device_id={"ctx": to}, device_id_type=MESH,
             ).start()
 
-        pltpu.make_async_copy(ret_send.at[c, me], ret_recv.at[c, me], rrecv_sem.at[c]).start()
+        ret_recv[c, me] = ret_send[c, me]
         pick = (((iota((16, SPAN), 1) >> 3) & 1) == iota((16, SPAN), 0)).astype(F32).astype(BF16)
         sums = mm(pick, k)[0:2]
         o_cent[c] = sums / jnp.sqrt(jnp.mean(sums * sums, axis=-1, keepdims=True) + EPSILON)
 
-    own_bias.wait()
-    pltpu.make_async_copy(
-        bias_a_recv.at[pl.ds(0, N_CTX - 1)], bias_a_recv.at[pl.ds(0, N_CTX - 1)], small_rsem.at[1]
-    ).wait()
-    bias_b[...] = jnp.sum(bias_a_recv[...], axis=0)
-
-    @pl.loop(1, N_HEAD)
-    def _(step):
-        pltpu.make_async_remote_copy(
-            bias_b, bias_b_recv.at[my_head], small_ssem.at[2], small_rsem.at[2],
-            device_id={"head": lax.rem(my_head + step, N_HEAD)}, device_id_type=MESH,
-        ).start()
-
-    own_sum = pltpu.make_async_copy(bias_b, bias_b_recv.at[my_head], self_sem.at[2])
-    own_sum.start()
+    @pl.when(lead)
+    def _():
+        landed(bias_b_recv.at[pl.ds(0, N_HEAD - 1)], small_rsem.at[2])
+        bias_c[...] = jnp.sum(bias_b_recv[...], axis=0)
+
+        @pl.loop(1, N_CTX)
+        def _(step):
+            pltpu.make_async_remote_copy(
+                bias_c, bias_d, small_ssem.at[3], small_rsem.at[3],
+                device_id={"ctx": peer(step)}, device_id_type=MESH,
+            ).start()
 
     for i in range(2):
         pltpu.make_async_remote_copy(
@@ -307,17 +333,11 @@
         ).wait_recv()
         wacc[i, pl.ds(TOK - WINDOW, WINDOW)] += grad_recv[i].astype(F32)
         (o_ldk, o_ldv)[i][...] = wacc[i].astype(BF16)
-    own_sum.wait()
-    pltpu.make_async_copy(
-        bias_b_recv.at[pl.ds(0, N_HEAD - 1)], bias_b_recv.at[pl.ds(0, N_HEAD - 1)], small_rsem.at[2]
-    ).wait()
-    o_bias[...] = jnp.sum(bias_b_recv[...], axis=0)
-
     acc[...] = jnp.zeros_like(acc)
 
     @pl.loop(0, CHUNKS)
     def _(c):
-        pltpu.make_async_copy(ret_recv.at[c], ret_recv.at[c], rrecv_sem.at[c]).wait()
+        landed(ret_recv.at[c, pl.ds(0, N_CTX - 1)], rrecv_sem.at[c])
         rows = jnp.concatenate([ret_recv[c, :, a].reshape(SPAN, DIM) for a in range(4)], axis=1)
         acc[...] += mm(back_hot[c], rows)
 
@@ -332,9 +352,19 @@
     for i in range(2):
         pltpu.make_async_copy(halo.at[i], halo.at[i], halo_ssem.at[i]).wait()
         pltpu.make_async_copy(grad_send.at[i], grad_send.at[i], grad_ssem.at[i]).wait()
-    for i, n in enumerate((N_CTX, N_CTX, N_HEAD)):
-        part = cnt_recv.at[pl.ds(0, n - 1)]
-        pltpu.make_async_copy(part, part, small_ssem.at[i]).wait()
+    landed(cnt_recv.at[pl.ds(0, N_CTX - 1)], small_ssem.at[0])
+
+    @pl.when(lead)
+    def _():
+        o_bias[...] = bias_c[...]
+        landed(bias_b_recv.at[pl.ds(0, N_HEAD - 1)], small_ssem.at[2])
+        landed(bias_a_recv.at[pl.ds(0, N_CTX - 1)], small_ssem.at[3])
+
+    @pl.when(me != 0)
+    def _():
+        landed(bias_d, small_rsem.at[3])
+        o_bias[...] = bias_d[...]
+        landed(bias_a, small_ssem.at[1])
 
 
 def deliver(*refs):
@@ -358,14 +388,14 @@
         vm((2, WINDOW, DIM), BF16), vm((2, WINDOW, DIM), BF16), vm((2, WINDOW, DIM), BF16),
         vm((1, DIM), F32), vm((N_CTX, 1, DIM), F32),
         vm((1, DIM), F32), vm((N_CTX, 1, DIM), F32),
-        vm((1, DIM), F32), vm((N_HEAD, 1, DIM), F32),
+        vm((1, DIM), F32), vm((N_HEAD, 1, DIM), F32), vm((1, DIM), F32), vm((1, DIM), F32),
         vm((1, TOK), I32), vm((CHUNKS, TOK, SPAN), BF16), vm((CHUNKS, 1, SPAN), F32),
         vm((SPAN, SPAN), F32), vm((WINDOW, 2 * WINDOW), F32), vm((TOK, 4 * DIM), F32),
         vm((2, TOK, DIM), F32),
         vm((WINDOW, 2 * WINDOW), F32),
         dma((8,)),
         dma((CHUNKS,)), dma((CHUNKS,)), dma((CHUNKS,)), dma((CHUNKS,)),
-        dma((2,)), dma((2,)), dma((2,)), dma((2,)), dma((3,)), dma((3,)), dma((3,)),
+        dma((2,)), dma((2,)), dma((2,)), dma((2,)), dma((4,)), dma((4,)), pltpu.SemaphoreType.REGULAR,
     ]
     anywhere = pl.BlockSpec(memory_space=pl.ANY)
     small = [jax.ShapeDtypeStruct((CHUNKS, 2, DIM), F32), jax.ShapeDtypeStruct((1, DIM), F32)]

time: 38.7 us -> 35.9 us (0.928)
  Pallas kernels: 36.5 us -> 33.7 us
    pallas_call x1, Pallas kernels: 35.4 us -> 32.7 us  [shards(): pl.pallas_call(kernel, out_shape=[token_out] * 8 + small, in_specs=[anywh...]
where the time goes in v3:
time: 35.9 us; the launch traced here: 35.7 us
  Pallas kernels  33.7 us (94%)
  local copies, waits for them, and re-layouts  1.34 us (4%)
  between operations  0.67 us (2%)
    pallas_call x1, Pallas kernels, shards(): pl.pallas_call(kernel, out_shape=[token_out] * 8 + small, in_specs=[anywh...  32.7 us
    unnamed x6, local copies, waits for them, and re-layouts  1.34 us
    pallas_call x1, Pallas kernels, shards(): pl.pallas_call(deliver, out_shape=[token_out] * 8 + small, in_specs=[anyw...  1.06 us

profile of v3, /device:TPU:0, one launch (start us, length us, event | category | flops | bytes accessed | tf_op | source)
XLA Modules:
  0.0 35.7 jit_solution(2273065339468141026)
XLA Ops:
  0.6 0.0 copy-start.2
  0.7 0.0 copy-start.1
  0.7 0.6 %copy-done.2 = f32[128]{0:T(128)S(1)} copy-done((f32[128]{0:T(128)S(1)}, f32[128]{0:T(128)}, u32[]{:S(2)}) %copy-start.2) | copy-done | bytes 536
  1.3 0.0 copy-done.1
  1.3 0.0 copy-start
  1.3 0.7 %copy-done = s32[1,512]{1,0:T(1,128)S(1)} copy-done((s32[1,512]{1,0:T(1,128)S(1)}, s32[1,512]{1,0:T(1,128)}, u32[]{:S(2)}) %copy-start) | copy-done | bytes 2072
  2.0 32.7 %routing.1 = (bf16[512,128]{1,0:T(8,128)(2,1)S(1)}, bf16[512,128]{1,0:T(8,128)(2,1)S(1)}, bf16[512,128]{1,0:T(8,128)(2,1)S(1)}, bf16[512,128]{1,0:T(8,128)(2,1)S...) custom-call(bf16[512,128]{1,0:T(8,128)(2,1)} %rq.1, ...), custom_call_target="tpu_custom_call" | custom-call | tf_op jit(solution)/shard_map/routing/pallas_call | solution.py:402
  34.7 1.1 %deliver.1 = (bf16[512,128]{1,0:T(8,128)(2,1)}, bf16[512,128]{1,0:T(8,128)(2,1)}, bf16[512,128]{1,0:T(8,128)(2,1)}, bf16[512,128]{1,0:T(8,128)(2,1)}, bf16[512,1...) custom-call(bf16[512,128]{1,0:T(8,128)(2,1)S(1)} %get-tuple-element., ...), custom_call_target="tpu_custom_call" | custom-call | tf_op jit(solution)/shard_map/deliver/pallas_call | solution.py:413
Async XLA Ops:
  0.6 0.7 %copy-start.2 = (f32[128]{0:T(128)S(1)}, f32[128]{0:T(128)}, u32[]{:S(2)}) copy-start(f32[128]{0:T(128)} %param.21) | copy-start | bytes 1540
  0.7 0.7 %copy-start.1 = (s32[1,128]{1,0:T(1,128)S(1)}, s32[1,128]{1,0:T(1,128)}, u32[]{:S(2)}) copy-start(s32[1,128]{1,0:T(1,128)} %slot.1) | copy-start | bytes 1540
  1.3 0.7 %copy-start = (s32[1,512]{1,0:T(1,128)S(1)}, s32[1,512]{1,0:T(1,128)}, u32[]{:S(2)}) copy-start(s32[1,512]{1,0:T(1,128)} %cl.1) | copy-start | bytes 6148

commit v4 on v3

--- a/solution.py
+++ b/solution.py
@@ -87,9 +87,9 @@
     lead = me == 0
     barrier = pltpu.get_barrier_semaphore()
 
-    @pl.loop(1, N_CTX)
-    def _(step):
-        to = peer(step)
+    @pl.loop(0, N_CTX - 1)
+    def _(i):
+        to = peer(lax.rem(i + 9, N_CTX - 1) + 1)
 
         @pl.when(to != 0)
         def _():
@@ -114,8 +114,8 @@
     local_in = [fetch(src, dst, 4 + i) for i, (src, dst) in enumerate(((lk, wk), (lv, wv), (lq, wq), (lg, wg)))]
 
     cluster_rows = iota((DIM, TOK), 0)
-    named = (cl[...] == cluster_rows).astype(F32).astype(BF16)
-    slots16 = jnp.broadcast_to(slot[...].astype(F32), (16, DIM)).astype(BF16)
+    named = (jnp.concatenate([cl[i] for i in range(4)], axis=1) == cluster_rows).astype(F32).astype(BF16)
+    slots16 = jnp.broadcast_to(slot[0].astype(F32), (16, DIM)).astype(BF16)
     slot_of = mm(slots16, named)[0:1].astype(I32)
     in_slot = slot_of == cluster_rows
     placed = in_slot.astype(F32).astype(BF16)
@@ -137,6 +137,8 @@
         for a in range(4):
             send[c, :, a] = rows[:, a * DIM : (a + 1) * DIM].reshape(N_CTX, ROWS, DIM)
 
+    pack(0)
+
     @pl.when(me != 0)
     def _():
         pl.semaphore_wait(barrier, N_CTX - 1)
@@ -155,19 +157,10 @@
             device_id={"ctx": ahead}, device_id_type=MESH,
         ).start()
 
-    @pl.loop(1, N_CTX)
-    def _(step):
-        pltpu.make_async_remote_copy(
-            cnt_send, cnt_recv.at[me], small_ssem.at[0], small_rsem.at[0],
-            device_id={"ctx": peer(step)}, device_id_type=MESH,
-        ).start()
-
     cnt_recv[me] = cnt_send[...]
 
     @pl.loop(0, CHUNKS)
     def _(c):
-        pack(c)
-
         @pl.loop(1, N_CTX)
         def _(step):
             to = peer(step)
@@ -176,7 +169,20 @@
                 device_id={"ctx": to}, device_id_type=MESH,
             ).start()
 
+        @pl.when(c == 0)
+        def _():
+            @pl.loop(1, N_CTX)
+            def _(step):
+                pltpu.make_async_remote_copy(
+                    cnt_send, cnt_recv.at[me], small_ssem.at[0], small_rsem.at[0],
+                    device_id={"ctx": peer(step)}, device_id_type=MESH,
+                ).start()
+
         recv[c, me] = send[c, me]
+
+        @pl.when(c < CHUNKS - 1)
+        def _():
+            pack(c + 1)
 
     back_hot[...] = jnp.zeros_like(back_hot)
     flat_col = jnp.transpose(jnp.broadcast_to(flat.astype(F32), (8, TOK)))[:, 0:1].astype(I32)
@@ -409,7 +415,7 @@
             collective_id=0, has_side_effects=True, vmem_limit_bytes=VMEM_GRANT
         ),
         name="routing",
-    )(rq, rk, rv, rg, lq, lk, lv, lg, clusters, cluster_slot, rel_bias.reshape(1, DIM))
+    )(rq, rk, rv, rg, lq, lk, lv, lg, clusters.reshape(4, 1, DIM), cluster_slot.reshape(1, 1, DIM), rel_bias.reshape(1, DIM))
     ro, rdq, rdk, rdv, lo, ldq, ldk, ldv, cent, bias = pl.pallas_call(
         deliver,
         out_shape=[token_out] * 8 + small,

time: 35.9 us -> 35.2 us (0.981)
  local copies, waits for them, and re-layouts: 1.34 us -> 0.66 us
    unnamed x6, local copies, waits for them, and re-layouts: 1.34 us -> 0.66 us
where the time goes in v4:
time: 35.2 us; the launch traced here: 34.9 us
  Pallas kernels  33.6 us (95%)
  between operations  0.68 us (2%)
  local copies, waits for them, and re-layouts  0.66 us (2%)
    pallas_call x1, Pallas kernels, shards(): pl.pallas_call(kernel, out_shape=[token_out] * 8 + small, in_specs=[anywh...  32.5 us
    pallas_call x1, Pallas kernels, shards(): pl.pallas_call(deliver, out_shape=[token_out] * 8 + small, in_specs=[anyw...  1.06 us

profile of v4, /device:TPU:0, one launch (start us, length us, event | category | flops | bytes accessed | tf_op | source)
XLA Modules:
  0.0 34.9 jit_solution(12907390566789864850)
XLA Ops:
  0.6 0.0 copy-start
  0.7 0.0 copy-start.1
  0.7 0.0 copy-start.2
  0.7 0.7 %copy-done = s32[1,512]{1,0:T(1,128)S(1)} copy-done((s32[1,512]{1,0:T(1,128)S(1)}, s32[1,512]{1,0:T(1,128)}, u32[]{:S(2)}) %copy-start) | copy-done | bytes 2072
  1.3 0.0 copy-done.1
  1.3 0.0 copy-done.2
  1.3 32.5 %routing.1 = (bf16[512,128]{1,0:T(8,128)(2,1)S(1)}, bf16[512,128]{1,0:T(8,128)(2,1)S(1)}, bf16[512,128]{1,0:T(8,128)(2,1)S(1)}, bf16[512,128]{1,0:T(8,128)(2,1)S...) custom-call(bf16[512,128]{1,0:T(8,128)(2,1)} %rq.1, ...), custom_call_target="tpu_custom_call" | custom-call | tf_op jit(solution)/shard_map/routing/pallas_call | solution.py:408
  33.8 1.1 %deliver.1 = (bf16[512,128]{1,0:T(8,128)(2,1)}, bf16[512,128]{1,0:T(8,128)(2,1)}, bf16[512,128]{1,0:T(8,128)(2,1)}, bf16[512,128]{1,0:T(8,128)(2,1)}, bf16[512,1...) custom-call(bf16[512,128]{1,0:T(8,128)(2,1)S(1)} %get-tuple-element., ...), custom_call_target="tpu_custom_call" | custom-call | tf_op jit(solution)/shard_map/deliver/pallas_call | solution.py:419
Async XLA Ops:
  0.6 0.7 %copy-start = (s32[1,512]{1,0:T(1,128)S(1)}, s32[1,512]{1,0:T(1,128)}, u32[]{:S(2)}) copy-start(s32[1,512]{1,0:T(1,128)} %param.19) | copy-start | bytes 6148
  0.7 0.7 %copy-start.1 = (s32[1,128]{1,0:T(1,128)S(1)}, s32[1,128]{1,0:T(1,128)}, u32[]{:S(2)}) copy-start(s32[1,128]{1,0:T(1,128)} %param.20) | copy-start | bytes 1540
  0.7 0.7 %copy-start.2 = (f32[128]{0:T(128)S(1)}, f32[128]{0:T(128)}, u32[]{:S(2)}) copy-start(f32[128]{0:T(128)} %param.21) | copy-start | bytes 1540

commit v5 on v4

--- a/solution.py
+++ b/solution.py
@@ -80,8 +80,10 @@
     behind = lax.rem(me + N_CTX - 1, N_CTX)
 
     def peer(step):
-        px = lax.rem(my_x + lax.rem(step, 4), 4)
-        py = lax.rem(my_y + lax.div(step, 4), 4)
+        low, high = lax.rem(step, 4), lax.div(step, 4)
+        odd = lax.rem(my_head, 2)
+        px = lax.rem(my_x + low + odd * (high - low), 4)
+        py = lax.rem(my_y + high + odd * (low - high), 4)
         return py * 4 + px
 
     lead = me == 0
@@ -151,12 +153,6 @@
 
     for copy in local_in[:2]:
         copy.wait()
-    for i, src in enumerate((wk, wv)):
-        pltpu.make_async_remote_copy(
-            src.at[pl.ds(TOK - WINDOW, WINDOW)], halo.at[i], halo_ssem.at[i], halo_rsem.at[i],
-            device_id={"ctx": ahead}, device_id_type=MESH,
-        ).start()
-
     cnt_recv[me] = cnt_send[...]
 
     @pl.loop(0, CHUNKS)
@@ -169,6 +165,16 @@
                 device_id={"ctx": to}, device_id_type=MESH,
             ).start()
 
+            @pl.when((c == 0) & (step <= WINDOW // ROWS))
+            def _():
+                piece = pl.ds(pl.multiple_of((step - 1) * ROWS, ROWS), ROWS)
+                tail = pl.ds(pl.multiple_of(TOK - WINDOW + (step - 1) * ROWS, ROWS), ROWS)
+                for i, src in enumerate((wk, wv)):
+                    pltpu.make_async_remote_copy(
+                        src.at[tail], halo.at[i, piece], halo_ssem.at[i], halo_rsem.at[i],
+                        device_id={"ctx": ahead}, device_id_type=MESH,
+                    ).start()
+
         @pl.when(c == 0)
         def _():
             @pl.loop(1, N_CTX)
@@ -184,7 +190,6 @@
         def _():
             pack(c + 1)
 
-    back_hot[...] = jnp.zeros_like(back_hot)
     flat_col = jnp.transpose(jnp.broadcast_to(flat.astype(F32), (8, TOK)))[:, 0:1].astype(I32)
 
     @pl.loop(0, CHUNKS)

time: 35.2 us -> 35.2 us (level)
  no operation moved by 1% of the time
where the time goes in v5:
time: 35.2 us; the launch traced here: 35 us
  Pallas kernels  33.6 us (95%)
  between operations  0.68 us (2%)
  local copies, waits for them, and re-layouts  0.66 us (2%)
    pallas_call x1, Pallas kernels, shards(): pl.pallas_call(kernel, out_shape=[token_out] * 8 + small, in_specs=[anywh...  32.6 us
    pallas_call x1, Pallas kernels, shards(): pl.pallas_call(deliver, out_shape=[token_out] * 8 + small, in_specs=[anyw...  1.06 us

profile of v5, /device:TPU:0, one launch (start us, length us, event | category | flops | bytes accessed | tf_op | source)
XLA Modules:
  0.0 35.0 jit_solution(4763488141834006218)
XLA Ops:
  0.6 0.0 copy-start
  0.7 0.0 copy-start.1
  0.7 0.0 copy-start.2
  0.7 0.7 %copy-done = s32[1,512]{1,0:T(1,128)S(1)} copy-done((s32[1,512]{1,0:T(1,128)S(1)}, s32[1,512]{1,0:T(1,128)}, u32[]{:S(2)}) %copy-start) | copy-done | bytes 2072
  1.3 0.0 copy-done.1
  1.3 0.0 copy-done.2
  1.3 32.6 %routing.1 = (bf16[512,128]{1,0:T(8,128)(2,1)S(1)}, bf16[512,128]{1,0:T(8,128)(2,1)S(1)}, bf16[512,128]{1,0:T(8,128)(2,1)S(1)}, bf16[512,128]{1,0:T(8,128)(2,1)S...) custom-call(bf16[512,128]{1,0:T(8,128)(2,1)} %rq.1, ...), custom_call_target="tpu_custom_call" | custom-call | tf_op jit(solution)/shard_map/routing/pallas_call | solution.py:413
  33.9 1.1 %deliver.1 = (bf16[512,128]{1,0:T(8,128)(2,1)}, bf16[512,128]{1,0:T(8,128)(2,1)}, bf16[512,128]{1,0:T(8,128)(2,1)}, bf16[512,128]{1,0:T(8,128)(2,1)}, bf16[512,1...) custom-call(bf16[512,128]{1,0:T(8,128)(2,1)S(1)} %get-tuple-element., ...), custom_call_target="tpu_custom_call" | custom-call | tf_op jit(solution)/shard_map/deliver/pallas_call | solution.py:424
Async XLA Ops:
  0.6 0.7 %copy-start = (s32[1,512]{1,0:T(1,128)S(1)}, s32[1,512]{1,0:T(1,128)}, u32[]{:S(2)}) copy-start(s32[1,512]{1,0:T(1,128)} %param.19) | copy-start | bytes 6148
  0.7 0.7 %copy-start.1 = (s32[1,128]{1,0:T(1,128)S(1)}, s32[1,128]{1,0:T(1,128)}, u32[]{:S(2)}) copy-start(s32[1,128]{1,0:T(1,128)} %param.20) | copy-start | bytes 1540
  0.7 0.7 %copy-start.2 = (f32[128]{0:T(128)S(1)}, f32[128]{0:T(128)}, u32[]{:S(2)}) copy-start(f32[128]{0:T(128)} %param.21) | copy-start | bytes 1540

commit v6 on v4

--- a/solution.py
+++ b/solution.py
@@ -16,6 +16,7 @@
 ROWS = 16
 SPAN = N_CTX * ROWS
 NEG = -1e30
+FAR_CORNER = 10
 EPSILON = 1e-06
 VMEM_GRANT = 54140 * 1024
 SCALE = DIM ** (-0.5)
@@ -142,11 +143,14 @@
     @pl.when(me != 0)
     def _():
         pl.semaphore_wait(barrier, N_CTX - 1)
+
+    @pl.when(me == FAR_CORNER)
+    def _():
         pl.semaphore_signal(go_sem, inc=1, device_id={"ctx": 0}, device_id_type=MESH)
 
     @pl.when(lead)
     def _():
-        pl.semaphore_wait(go_sem, N_CTX - 1)
+        pl.semaphore_wait(go_sem, 1)
 
 
     for copy in local_in[:2]:

time: 35.2 us -> 35.2 us (level)
  no operation moved by 1% of the time
where the time goes in v6:
time: 35.2 us; the launch traced here: 34.9 us
  Pallas kernels  33.6 us (95%)
  between operations  0.68 us (2%)
  local copies, waits for them, and re-layouts  0.66 us (2%)
    pallas_call x1, Pallas kernels, shards(): pl.pallas_call(kernel, out_shape=[token_out] * 8 + small, in_specs=[anywh...  32.5 us
    pallas_call x1, Pallas kernels, shards(): pl.pallas_call(deliver, out_shape=[token_out] * 8 + small, in_specs=[anyw...  1.06 us

profile of v6, /device:TPU:0, one launch (start us, length us, event | category | flops | bytes accessed | tf_op | source)
XLA Modules:
  0.0 34.9 jit_solution(13996478902976788242)
XLA Ops:
  0.6 0.0 copy-start
  0.7 0.0 copy-start.1
  0.7 0.0 copy-start.2
  0.7 0.7 %copy-done = s32[1,512]{1,0:T(1,128)S(1)} copy-done((s32[1,512]{1,0:T(1,128)S(1)}, s32[1,512]{1,0:T(1,128)}, u32[]{:S(2)}) %copy-start) | copy-done | bytes 2072
  1.3 0.0 copy-done.1
  1.3 0.0 copy-done.2
  1.3 32.5 %routing.1 = (bf16[512,128]{1,0:T(8,128)(2,1)S(1)}, bf16[512,128]{1,0:T(8,128)(2,1)S(1)}, bf16[512,128]{1,0:T(8,128)(2,1)S(1)}, bf16[512,128]{1,0:T(8,128)(2,1)S...) custom-call(bf16[512,128]{1,0:T(8,128)(2,1)} %rq.1, ...), custom_call_target="tpu_custom_call" | custom-call | tf_op jit(solution)/shard_map/routing/pallas_call | solution.py:412
  33.8 1.1 %deliver.1 = (bf16[512,128]{1,0:T(8,128)(2,1)}, bf16[512,128]{1,0:T(8,128)(2,1)}, bf16[512,128]{1,0:T(8,128)(2,1)}, bf16[512,128]{1,0:T(8,128)(2,1)}, bf16[512,1...) custom-call(bf16[512,128]{1,0:T(8,128)(2,1)S(1)} %get-tuple-element., ...), custom_call_target="tpu_custom_call" | custom-call | tf_op jit(solution)/shard_map/deliver/pallas_call | solution.py:423
Async XLA Ops:
  0.6 0.7 %copy-start = (s32[1,512]{1,0:T(1,128)S(1)}, s32[1,512]{1,0:T(1,128)}, u32[]{:S(2)}) copy-start(s32[1,512]{1,0:T(1,128)} %param.19) | copy-start | bytes 6148
  0.7 0.7 %copy-start.1 = (s32[1,128]{1,0:T(1,128)S(1)}, s32[1,128]{1,0:T(1,128)}, u32[]{:S(2)}) copy-start(s32[1,128]{1,0:T(1,128)} %param.20) | copy-start | bytes 1540
  0.7 0.7 %copy-start.2 = (f32[128]{0:T(128)S(1)}, f32[128]{0:T(128)}, u32[]{:S(2)}) copy-start(f32[128]{0:T(128)} %param.21) | copy-start | bytes 1540
